TPU v7x, 32 devices: a whole 2x2x4 slice. The times are simulated.
32 devices in a mesh: dp: 8 (over y, x, core), head: 4 (over z).
Axes of the slice: x: 2, y: 2, z: 4, core: 2. Of those that a mesh axis runs over, the one named last changes fastest.
Arguments:
- tokens: bfloat16 [512, 32, 768], P('head', 'dp'), may hold values from -6 to 6
- lengths: int32 [32], P('dp'), may hold values from 20 to 512, as said below
- ranges: int32 [4], replicated, may hold values from 32 to 96
- qkv_weight: bfloat16 [3, 768, 768], replicated, may hold values from -0.21875 to 0.21875
- qv_bias: bfloat16 [2, 768], replicated, may hold values from -1.796875 to 1.796875
- out_weight: bfloat16 [768, 768], replicated, may hold values from -1.75 to 1.75
- out_bias: bfloat16 [768], replicated, may hold values from -1.796875 to 1.796875
- norm_gains: bfloat16 [2, 768], replicated, may hold values from 0.5 to 1.5
- norm_shifts: bfloat16 [2, 768], replicated, may hold values from -1.796875 to 1.796875
- ffn_in: bfloat16 [768, 3072], replicated, may hold values from -0.21875 to 0.21875
- ffn_in_bias: bfloat16 [3072], replicated, may hold values from -1.796875 to 1.796875
- ffn_out: bfloat16 [3072, 768], replicated, may hold values from -0.109375 to 0.109375
- ffn_out_bias: bfloat16 [768], replicated, may hold values from -1.796875 to 1.796875
- cotangent: bfloat16 [512, 32, 768], P('head', 'dp'), may hold values from -6 to 6
Outputs:
- output: bfloat16 [512, 32, 768], P('head', 'dp')
- grad_tokens: float32 [512, 32, 768], P('head', 'dp')
- grad_qkv_weight: float32 [3, 768, 768], P(None, 'dp')
- grad_qv_bias: float32 [2, 768], P(None, 'dp')
- grad_out_weight: float32 [768, 768], P('dp')
- grad_out_bias: float32 [768], P('dp')
- grad_norm_gains: float32 [2, 768], P(None, 'dp')
- grad_norm_shifts: float32 [2, 768], P(None, 'dp')
- grad_ffn_in: float32 [768, 3072], P('dp')
- grad_ffn_in_bias: float32 [3072], P('dp')
- grad_ffn_out: float32 [3072, 768], P('dp')
- grad_ffn_out_bias: float32 [768], P('dp')
Inputs may be any that keep to these rules, and one draw needn't show every extreme that they name: `lengths`: in every group of 4 consecutive sequences one has exactly 512 tokens.
All inputs are finite; a program needn't handle non-finite values.
Results may differ from a plain program's by a relative error of at most 0.017.
Values may be sent and summed in bfloat16 or wider, within the bound.
A program may use at most 192 MiB of HBM per device.

v0:
```python
import jax
import jax.numpy as jnp
from jax import lax
from jax.sharding import PartitionSpec as P

HEAD_DIM = 64


def soft_clip(value, bound):
    return bound * jnp.tanh(value / bound)


def clip_slope(value, bound):
    inner = jnp.tanh(value / bound)
    return 1.0 - inner * inner


def layer_norm(value, gain, shift):
    center = value - jnp.mean(value, axis=-1, keepdims=True)
    spread = jnp.mean(center * center, axis=-1, keepdims=True)
    return center * lax.rsqrt(spread + 1e-05) * gain + shift


def split_heads(stacked):
    length = stacked.shape[1]
    heads_here = stacked.shape[2] // HEAD_DIM
    return (
        stacked[0].reshape(length, heads_here, HEAD_DIM),
        stacked[1].reshape(length, heads_here, HEAD_DIM),
        stacked[2].reshape(length, heads_here, HEAD_DIM),
    )


def masked_scores(queries, key_rows, length):
    scores = jnp.einsum(
        "ihe,jhe->hij", queries, key_rows, preferred_element_type=jnp.float32
    ) * HEAD_DIM ** (-0.5)
    live = jnp.arange(queries.shape[0]) < length
    return jnp.where(live[None, None, :], scores, -1000000000.0)


def attend_forward(pieces):
    stacked, length = pieces
    queries, key_rows, values = split_heads(stacked)
    masked = masked_scores(queries, key_rows, length)
    highest = jnp.max(masked, axis=-1, keepdims=True)
    exponent = jnp.exp(masked - highest)
    totals = jnp.sum(exponent, axis=-1, keepdims=True)
    probs = exponent / totals
    log_totals = (highest + jnp.log(totals))[:, :, 0]
    context = jnp.einsum(
        "hij,jhe->ihe", probs.astype(jnp.bfloat16), values, preferred_element_type=jnp.float32
    )
    return (context.astype(jnp.bfloat16).reshape(stacked.shape[1], stacked.shape[2]), log_totals)


def attend_backward(pieces):
    stacked, length, log_totals, grad_context = pieces
    queries, key_rows, values = split_heads(stacked)
    grad_ctx = grad_context.reshape(queries.shape)
    masked = masked_scores(queries, key_rows, length)
    probs = jnp.exp(masked - log_totals[:, :, None])
    probs_low = probs.astype(jnp.bfloat16)
    grad_probs = jnp.einsum("ihe,jhe->hij", grad_ctx, values, preferred_element_type=jnp.float32)
    grad_values = jnp.einsum(
        "hij,ihe->jhe", probs_low, grad_ctx, preferred_element_type=jnp.float32
    )
    delta = jnp.sum(grad_probs * probs, axis=-1, keepdims=True)
    grad_scores = (probs * (grad_probs - delta)).astype(jnp.bfloat16)
    scale = HEAD_DIM ** (-0.5)
    grad_queries = (
        jnp.einsum("hij,jhe->ihe", grad_scores, key_rows, preferred_element_type=jnp.float32)
        * scale
    )
    grad_keys = (
        jnp.einsum("hij,ihe->jhe", grad_scores, queries, preferred_element_type=jnp.float32) * scale
    )
    shape_two = (stacked.shape[1], stacked.shape[2])
    return jnp.stack(
        [
            grad_queries.reshape(shape_two),
            grad_keys.reshape(shape_two),
            grad_values.reshape(shape_two),
        ]
    ).astype(jnp.bfloat16)


def on_device(
    tokens,
    lengths,
    ranges,
    qkv_weight,
    qv_bias,
    out_weight,
    out_bias,
    norm_gains,
    norm_shifts,
    ffn_in,
    ffn_in_bias,
    ffn_out,
    ffn_out_bias,
    cotangent,
):
    bounds = ranges.astype(jnp.float32) / 16.0
    inputs = tokens.astype(jnp.float32)
    gains = norm_gains.astype(jnp.float32)
    shifts = norm_shifts.astype(jnp.float32)
    quant_in = soft_clip(inputs, bounds[0]).astype(jnp.bfloat16)
    projected = jnp.einsum(
        "psd,ide->sipe", quant_in, qkv_weight, preferred_element_type=jnp.float32
    )
    qv_float = qv_bias.astype(jnp.float32)
    bias_rows = jnp.stack([qv_float[0], jnp.zeros_like(qv_float[0]), qv_float[1]])
    projected = (projected + bias_rows[None, :, None, :]).astype(jnp.bfloat16)
    per_head = lax.all_to_all(projected, "head", split_axis=3, concat_axis=2, tiled=True)
    context, log_totals = lax.map(attend_forward, (per_head, lengths))
    ctx_tokens = lax.all_to_all(context, "head", split_axis=1, concat_axis=2, tiled=True).astype(
        jnp.float32
    )
    quant_ctx = soft_clip(ctx_tokens, bounds[1]).astype(jnp.bfloat16)
    attn_out = jnp.einsum("spd,de->pse", quant_ctx, out_weight, preferred_element_type=jnp.float32)
    attn_out = attn_out + out_bias.astype(jnp.float32)
    hidden, first_back = jax.vjp(layer_norm, inputs + attn_out, gains[0], shifts[0])
    quant_h = soft_clip(hidden, bounds[2]).astype(jnp.bfloat16)
    pre = jnp.einsum("psd,df->psf", quant_h, ffn_in, preferred_element_type=jnp.float32)
    pre = pre + ffn_in_bias.astype(jnp.float32)

    def activate(value):
        return soft_clip(jax.nn.gelu(value, approximate=True), bounds[3])

    act_float, act_back = jax.vjp(activate, pre)
    act = act_float.astype(jnp.bfloat16)
    branch = jnp.einsum("psf,fd->psd", act, ffn_out, preferred_element_type=jnp.float32)
    branch = branch + ffn_out_bias.astype(jnp.float32)
    normed, second_back = jax.vjp(layer_norm, hidden + branch, gains[1], shifts[1])
    output = normed.astype(jnp.bfloat16)
    grad_sum2, gain_two, shift_two = second_back(cotangent.astype(jnp.float32))
    grad_branch = grad_sum2.astype(jnp.bfloat16)
    grad_ffn_out = jnp.einsum("psf,psd->fd", act, grad_branch, preferred_element_type=jnp.float32)
    grad_ffn_out_bias = jnp.sum(grad_branch.astype(jnp.float32), axis=(0, 1))
    grad_act = jnp.einsum("psd,fd->psf", grad_branch, ffn_out, preferred_element_type=jnp.float32)
    grad_pre = act_back(grad_act)[0].astype(jnp.bfloat16)
    grad_ffn_in = jnp.einsum("psd,psf->df", quant_h, grad_pre, preferred_element_type=jnp.float32)
    grad_ffn_in_bias = jnp.sum(grad_pre.astype(jnp.float32), axis=(0, 1))
    grad_quant_h = jnp.einsum("psf,df->psd", grad_pre, ffn_in, preferred_element_type=jnp.float32)
    grad_hidden = grad_sum2 + grad_quant_h * clip_slope(hidden, bounds[2])
    grad_sum1, gain_one, shift_one = first_back(grad_hidden)
    grad_attn = grad_sum1.astype(jnp.bfloat16)
    grad_out_weight = jnp.einsum(
        "spd,pse->de", quant_ctx, grad_attn, preferred_element_type=jnp.float32
    )
    grad_out_bias = jnp.sum(grad_attn.astype(jnp.float32), axis=(0, 1))
    grad_norm_gains = jnp.stack([gain_one, gain_two])
    grad_norm_shifts = jnp.stack([shift_one, shift_two])
    grad_quant_ctx = jnp.einsum(
        "pse,de->spd", grad_attn, out_weight, preferred_element_type=jnp.float32
    )
    grad_context = (grad_quant_ctx * clip_slope(ctx_tokens, bounds[1])).astype(jnp.bfloat16)
    grad_heads = lax.all_to_all(grad_context, "head", split_axis=2, concat_axis=1, tiled=True)
    grad_stack = lax.map(attend_backward, (per_head, lengths, log_totals, grad_heads))
    grad_projected = lax.all_to_all(grad_stack, "head", split_axis=2, concat_axis=3, tiled=True)
    grad_qkv_weight = jnp.einsum(
        "psd,sipe->ide", quant_in, grad_projected, preferred_element_type=jnp.float32
    )
    grad_float = grad_projected.astype(jnp.float32)
    grad_qv_bias = jnp.stack(
        [jnp.sum(grad_float[:, 0], axis=(0, 1)), jnp.sum(grad_float[:, 2], axis=(0, 1))]
    )
    grad_quant_in = jnp.einsum(
        "sipe,ide->psd", grad_projected, qkv_weight, preferred_element_type=jnp.float32
    )
    grad_tokens = grad_sum1 + grad_quant_in * clip_slope(inputs, bounds[0])
    shares = (
        lax.psum_scatter(grad_qkv_weight, "dp", scatter_dimension=1, tiled=True),
        lax.psum_scatter(grad_qv_bias, "dp", scatter_dimension=1, tiled=True),
        lax.psum_scatter(grad_out_weight, "dp", scatter_dimension=0, tiled=True),
        lax.psum_scatter(grad_out_bias, "dp", scatter_dimension=0, tiled=True),
        lax.psum_scatter(grad_norm_gains, "dp", scatter_dimension=1, tiled=True),
        lax.psum_scatter(grad_norm_shifts, "dp", scatter_dimension=1, tiled=True),
        lax.psum_scatter(grad_ffn_in, "dp", scatter_dimension=0, tiled=True),
        lax.psum_scatter(grad_ffn_in_bias, "dp", scatter_dimension=0, tiled=True),
        lax.psum_scatter(grad_ffn_out, "dp", scatter_dimension=0, tiled=True),
        lax.psum_scatter(grad_ffn_out_bias, "dp", scatter_dimension=0, tiled=True),
    )
    summed = tuple(
        (
            lax.psum(shares[0].astype(jnp.bfloat16), "head").astype(jnp.float32),
            lax.psum(shares[1].astype(jnp.bfloat16), "head").astype(jnp.float32),
            lax.psum(shares[2].astype(jnp.bfloat16), "head").astype(jnp.float32),
            lax.psum(shares[3].astype(jnp.bfloat16), "head").astype(jnp.float32),
            lax.psum(shares[4].astype(jnp.bfloat16), "head").astype(jnp.float32),
            lax.psum(shares[5].astype(jnp.bfloat16), "head").astype(jnp.float32),
            lax.psum(shares[6].astype(jnp.bfloat16), "head").astype(jnp.float32),
            lax.psum(shares[7].astype(jnp.bfloat16), "head").astype(jnp.float32),
            lax.psum(shares[8].astype(jnp.bfloat16), "head").astype(jnp.float32),
            lax.psum(shares[9].astype(jnp.bfloat16), "head").astype(jnp.float32),
        )
    )
    return (
        output,
        grad_tokens,
        summed[0],
        summed[1],
        summed[2],
        summed[3],
        summed[4],
        summed[5],
        summed[6],
        summed[7],
        summed[8],
        summed[9],
    )


def solution(mesh):
    placed = (
        P("head", "dp", None),
        P("dp"),
        P(),
        P(),
        P(),
        P(),
        P(),
        P(),
        P(),
        P(),
        P(),
        P(),
        P(),
        P("head", "dp", None),
    )
    return jax.shard_map(
        on_device,
        mesh=mesh,
        in_specs=placed,
        out_specs=(
            P("head", "dp", None),
            P("head", "dp", None),
            P(None, "dp", None),
            P(None, "dp"),
            P("dp", None),
            P("dp"),
            P(None, "dp"),
            P(None, "dp"),
            P("dp", None),
            P("dp"),
            P("dp", None),
            P("dp"),
        ),
        check_vma=False,
    )
```

profile of v0, /device:TPU:0, one launch (start us, length us, event | category | flops | bytes accessed | tf_op | source)
XLA Modules:
  0.0 675.6 jit_solution(10127624107865781532)
XLA Ops:
  9.5 5.2 fusion.31
  14.7 5.4 copy.143
  20.1 6.3 all-to-all-start
  26.5 53.9 %all-to-all-done = bf16[4,3,128,768]{2,0,1,3:T(4,128)(2,1)} async-done(((bf16[4,3,128,768]{2,0,1,3:T(4,128)(2,1)}), bf16[4,3,128,768]{2,0,1,3:T(4,128)(2,1)}, u32[]{:S(2)}, u32[]{:S(2)}) %all-to-all-start) | async-done | bytes 2359328 | tf_op jit(solution)/shard_map/all_to_all | solution.py:115
  80.4 2.1 copy.144
  84.4 24.7 %while.22 = (s32[]{:T(128)}, bf16[4,512,192]{1,2,0:T(8,128)(2,1)}, f32[4,3,512]{2,1,0:T(4,128)}, bf16[4,3,512,192]{2,3,1,0:T(8,128)(2,1)}, s32[4]{0:T(128)S(1)}, /*index=5*/s32[]{:T(128)}, s32[]{:T(128)}, s32[]{}, s32[]{}) while((s32[]{:T(128)}, bf16[4,512,192]{1,2,0:T(8,128)(2,1)}, f32[4,3,512]{2,1,0:T(4,128)}, ...), condition=%wide.region_3.4_spmd, body=%wide.region_0.3_spmd.sunk | while | flops 210861056 | bytes 11849889 | solution.py:116
  109.0 2.4 copy.146
  111.4 4.2 all-to-all-start.1
  119.8 21.2 %all-to-all-done.1 = bf16[4,512,192]{2,0,1:T(4,128)(2,1)} async-done(((bf16[4,512,192]{2,0,1:T(4,128)(2,1)}), bf16[4,512,192]{2,0,1:T(4,128)(2,1)}, u32[]{:S(2)}, u32[]{:S(2)}) %all-to-all-start.1) | async-done | bytes 786464 | tf_op jit(solution)/shard_map/all_to_all | solution.py:117
  140.9 2.4 copy.147
  143.3 3.5 multiply_subtract_fusion
  146.8 2.4 reshape.216
  153.5 6.1 fusion.25
  159.6 9.6 %fusion.59 = (f32[128,4]{0,1:T(4,128)S(1)}, f32[128,4,768]{2,0,1:T(8,128)S(1)}) fusion(f32[768]{0:T(1024)S(1)} %copy-done.19, bf16[3072,768]{1,0:T(8,128)(2,1)} %param.29, f32[]{:T(128)} %bitcast.31, f32[128,4,3072]{2,0,1:T(8,128)S(1)} %fusion.25, f32[3072]{0:T(1024)S(1)} %copy-done.13, f32[768]{0:T(1024)S(1)} %copy-done.18, ...), kind=kOutput, calls=%fused_computation.129 | convolution fusion | flops 2437545472 | bytes 14183428 | tf_op jit(solution)/shard_map/psf,fd->psd/dot_general | solution.py:133
  172.8 10.1 %convert_reduce_fusion = (f32[3072]{0:T(1024)}, bf16[128,4,3072]{2,0,1:T(8,128)(2,1)S(1)}) fusion(f32[128,4,3072]{2,0,1:T(8,128)S(1)} %fusion.25, f32[3072]{0:T(1024)S(1)} %copy-done.13, bf16[128,4,768]{2,0,1:T(8,128)(2,1)S(1)} %get-tuple-element.197, bf16[3072,768]{1,0:T(8,128)(2,1)S(1)} %bitcast.249, f32[]{:T(128)} %bitcast.31), kind=kOutput, calls=%fused_computation.41 | convolution fusion | flops 2464674816 | bytes 14966788 | tf_op jit(solution)/shard_map/psd,fd->psf/dot_general | solution.py:141
  182.9 4.9 multiply_reduce_fusion.1
  190.6 2.2 convolution_bitcast_fusion.3
  192.9 11.7 %convolution_bitcast_fusion = f32[3072,768]{1,0:T(8,128)} fusion(bf16[128,4,768]{2,0,1:T(8,128)(2,1)} %copy-done.6, f32[]{:T(128)} %bitcast.31, f32[128,4,3072]{2,0,1:T(8,128)} %copy-done.25, f32[3072]{0:T(1024)} %convert_element_type.170), kind=kOutput, calls=%fused_computation.44 | convolution fusion | flops 2434793472 | bytes 16527364 | tf_op jit(solution)/shard_map/psf,psd->fd/dot_general | solution.py:139
  204.7 3.2 reshape.218
  207.9 2.7 copy.151
  210.6 3.0 copy.152
  213.7 3.7 fusion.40
  217.4 2.2 copy.153
  219.5 4.2 all-to-all-start.2
  223.8 9.5 %convolution_bitcast_fusion.1 = f32[768,3072]{1,0:T(8,128)} fusion(bf16[128,4,3072]{2,0,1:T(8,128)(2,1)} %copy-done.24, f32[]{:T(128)} %bitcast.32, f32[128,4,768]{2,0,1:T(8,128)} %copy-done.1, f32[768]{0:T(1024)} %get-tuple-element.160, f32[768]{0:T(1024)S(1)} %copy-done.12, f32[128,4]{0,1:T(4,128)} %copy-done.14, f32[128,4]{0,1:T(4,128)S(1)} %broadcast_multiply_fusion.1), kind=kOutput, calls=%fused_computation.45 | convolution fusion | flops 2418671616 | bytes 14166020 | tf_op jit(solution)/shard_map/psd,psf->df/dot_general | solution.py:143
  233.4 10.4 %all-to-all-done.2 = bf16[4,128,768]{1,0,2:T(4,128)(2,1)} async-done(((bf16[4,128,768]{1,0,2:T(4,128)(2,1)}), bf16[4,128,768]{1,0,2:T(4,128)(2,1)}, u32[]{:S(2)}, u32[]{:S(2)}) %all-to-all-start.2) | async-done | bytes 786464 | tf_op jit(solution)/shard_map/all_to_all | solution.py:159
  246.2 36.1 %while.23 = (s32[]{:T(128)}, bf16[4,3,512,192]{2,3,1,0:T(8,128)(2,1)}, bf16[4,3,512,192]{2,3,1,0:T(8,128)(2,1)}, s32[4]{0:T(128)S(1)}, f32[4,3,512]{2,1,0:T(4,12...) while((s32[]{:T(128)}, bf16[4,3,512,192]{2,3,1,0:T(8,128)(2,1)}, ...), condition=%wide.region_14.15_spmd, body=%wide.region_12.14_spmd.sunk | while | flops 512654336 | bytes 28343468 | solution.py:160
  282.3 5.8 copy.156
  288.1 75.6 %all_to_all.63 = bf16[4,3,512,192]{3,0,1,2:T(4,128)(2,1)} all-to-all(bf16[4,3,512,192]{3,0,1,2:T(4,128)(2,1)} %copy.156), channel_id=1, replica_groups=mesh['dp'=8,'head'=4] {'head'}, dimensions={2} | all-to-all | bytes 4718592 | tf_op jit(solution)/shard_map/all_to_all | solution.py:161
  363.7 5.7 copy.158
  369.4 7.5 %convolution_bitcast_fusion.2 = f32[3,768,768]{1,2,0:T(8,128)} fusion(bf16[4,3,128,768]{2,3,1,0:T(8,128)(2,1)} %bitcast.228, f32[]{:T(128)} %bitcast.20, bf16[128,4,768]{2,1,0:T(4,128)(2,1)} %param.18), kind=kOutput, calls=%fused_computation.58 | convolution fusion | flops 1813512192 | bytes 10223620 | tf_op jit(solution)/shard_map/psd,sipe->ide/dot_general | solution.py:162
  376.9 10.5 %copy.177 = f32[3,768,768]{2,0,1:T(4,128)} copy(f32[3,768,768]{1,2,0:T(8,128)} %convolution_bitcast_fusion.2) | data formatting | bytes 14155776
  387.4 8.3 %copy.187 = f32[96,8,3,768]{3,1,2,0:T(8,128)} copy(f32[96,8,3,768]{3,2,1,0:T(4,128)} %bitcast.214) | data formatting | bytes 14155776
  406.8 2.4 convert_element_type.198
  409.1 2.4 convert_element_type.193
  411.5 53.3 %reduce-scatter.22.cloned.1.call-done = f32[96,2304]{1,0:T(8,128)} async-done(((f32[768,2304]{1,0:T(8,128)}), f32[96,2304]{1,0:T(8,128)}) %reduce-scatter.22.cloned.1.call-update) | async-done | bytes 884752
  464.8 2.3 reshape.230
  467.0 2.1 copy.178
  471.1 2.6 copy.162
  473.7 23.7 %all-reduce.3 = (bf16[768]{0:T(1024)(128)(2,1)}, bf16[3072]{0:T(1024)(128)(2,1)}, bf16[768]{0:T(1024)(128)(2,1)S(1)}) all-reduce(f32[768]{0:T(1024)S(1)} %get-tuple-element.198, f32[3072]{0:T(1024)} %get-tuple-element.228, f32[768]{0:T(1024)S(1)} %get-tuple-element.196), channel_id=5, replica_groups=mesh['dp'=8,'head'=4] {'dp'}, use_global_device_ids=true, to_apply=%region_24.25.clone | all-reduce | flops 4608 | bytes 27648
  502.4 36.5 %reduce-scatter.26.cloned.1.call-done = f32[96,2]{1,0:T(8,128)} async-done(((f32[768,2]{1,0:T(8,128)}), f32[96,2]{1,0:T(8,128)}) %reduce-scatter.26.cloned.1.call-update) | async-done | bytes 784
  539.8 5.2 fusion.39
  545.0 2.2 copy.163
  547.1 28.7 %reduce-scatter.24.cloned.1.call-done = f32[96,2]{1,0:T(8,128)} async-done(((f32[768,2]{1,0:T(8,128)}), f32[96,2]{1,0:T(8,128)}) %reduce-scatter.24.cloned.1.call-update) | async-done | bytes 784
  576.7 12.5 %all-reduce.4 = (bf16[2,96]{1,0:T(2,128)(2,1)}, bf16[96]{0:T(256)(128)(2,1)}, bf16[2,96]{1,0:T(2,128)(2,1)}, bf16[2,96]{1,0:T(2,128)(2,1)}, bf16[384]{0:T(512)(128)(2,1)}, /*index=5*/bf16[96]{0:T(256)(128)(2,1)}) all-reduce(bf16[2,96]{1,0:T(2,128)(2,1)S(1)} %copy.180, ...), channel_id=1, replica_groups=mesh['dp'=8,'head'=4] {'head'}, use_global_device_ids=true, to_apply=%region_20.21 | all-reduce | flops 1152 | bytes 4608 | tf_op jit(solution)/shard_map/psum | solution.py:188
  596.5 64.8 %all-reduce.8.cloned.1.call-done = (bf16[3,96,768]{1,2,0:T(8,128)(2,1)}, bf16[96,768]{1,0:T(8,128)(2,1)}, bf16[96,3072]{1,0:T(8,128)(2,1)}, bf16[384,768]{1,0:T(8,128)(2,1)}) async-done(((bf16[3,96,768]{1,2,0:T(8,128)(2,1)}, bf16[96,768]{1,0:T(8,128)(2,1)}, bf16[96,3072]{1,0:T(8,128)(2,1)}, bf16[384,768]{1,0:T(8,128)(2,1)}), (bf16[3,96,768]{1,2,0:T(8,128)(2,1)}, bf16[96,768]{1,0:T(8,128)(2,1)}, ...) | async-done | bytes 1769488 | tf_op jit(solution)/shard_map/psum | solution.py:187
  661.4 2.2 copy.164
  665.3 2.2 convert_element_type.194
  (224 shorter events, 110.4 us)
Async XLA Ops:
  7.2 2.3 copy-start
  20.1 60.2 %all-to-all-start = ((bf16[4,3,128,768]{2,0,1,3:T(4,128)(2,1)}), bf16[4,3,128,768]{2,0,1,3:T(4,128)(2,1)}, u32[]{:S(2)}, u32[]{:S(2)}) async-start(bf16[4,3,128,768]{2,0,1,3:T(4,128)(2,1)} %copy.143), calls=%async_computation | async-start | bytes 4718592 | tf_op jit(solution)/shard_map/all_to_all | solution.py:115
  82.5 1.9 copy-start.21
  109.0 8.8 %copy-start.20 = (bf16[2,768]{1,0:T(2,128)(2,1)S(1)}, bf16[2,768]{1,0:T(2,128)(2,1)}, u32[]{:S(2)}) copy-start(bf16[2,768]{1,0:T(2,128)(2,1)} %param.25) | copy-start | bytes 9220
  109.0 9.5 %copy-start.17 = (bf16[3072]{0:T(1024)(128)(2,1)S(1)}, bf16[3072]{0:T(1024)(128)(2,1)}, u32[]{:S(2)}) copy-start(bf16[3072]{0:T(1024)(128)(2,1)} %param.28) | copy-start | bytes 18436
  111.4 29.5 %all-to-all-start.1 = ((bf16[4,512,192]{2,0,1:T(4,128)(2,1)}), bf16[4,512,192]{2,0,1:T(4,128)(2,1)}, u32[]{:S(2)}, u32[]{:S(2)}) async-start(bf16[4,512,192]{2,0,1:T(4,128)(2,1)} %copy.146), calls=%async_computation.1 | async-start | bytes 2097152 | tf_op jit(solution)/shard_map/all_to_all | solution.py:117
  115.6 289.5 %reduce-scatter.16.cloned.1.call-start = ((), (), s32[]{:S(2)}) async-start(), calls=%async_computation.11 | async-start | bytes 2654208 | tf_op jit(solution)/shard_map/reduce_scatter | solution.py:176
  119.8 39.8 %copy-start.10 = (f32[768]{0:T(1024)}, f32[768]{0:T(1024)S(1)}, u32[]{:S(2)}) copy-start(f32[768]{0:T(1024)S(1)} %get-tuple-element.230) | copy-start | bytes 9220
  149.3 1.5 copy-start.5
  152.8 35.0 %copy-start.1 = (f32[128,4,768]{2,0,1:T(8,128)}, f32[128,4,768]{2,0,1:T(8,128)S(1)}, u32[]{:S(2)}) copy-start(f32[128,4,768]{2,0,1:T(8,128)S(1)} %get-tuple-element.224) | copy-start | bytes 4718596
  152.8 0.7 copy-start.18
  153.2 34.6 %copy-start.14 = (f32[128,4]{0,1:T(4,128)}, f32[128,4]{0,1:T(4,128)S(1)}, u32[]{:S(2)}) copy-start(f32[128,4]{0,1:T(4,128)S(1)} %fusion.52) | copy-start | bytes 6148
  153.5 6.1 copy-start.13
  153.5 6.1 copy-start.19
  153.5 19.3 %slice-start = ((s8[4718592]{0:T(1024)(128)(4,1)}), s8[4194304]{0:T(1024)(128)(4,1)S(1)}, s32[]{:S(2)}) async-start(s8[4718592]{0:T(1024)(128)(4,1)} %bitcast.248), calls=%async_computation.19 | async-start | bytes 8388608
  159.6 13.2 %copy-start.25 = (f32[128,4,3072]{2,0,1:T(8,128)}, f32[128,4,3072]{2,0,1:T(8,128)S(1)}, u32[]{:S(2)}) copy-start(f32[128,4,3072]{2,0,1:T(8,128)S(1)} %fusion.25) | copy-start | bytes 18874372
  159.6 9.6 %copy-start.2 = (bf16[128,4,768]{2,1,0:T(4,128)(2,1)S(1)}, bf16[128,4,768]{2,1,0:T(4,128)(2,1)}, u32[]{:S(2)}) copy-start(bf16[128,4,768]{2,1,0:T(4,128)(2,1)} %param.31) | copy-start | bytes 2359300
  159.6 13.1 %slice-start.1 = ((s8[4718592]{0:T(1024)(128)(4,1)}), s8[524288]{0:T(1024)(128)(4,1)S(1)}, s32[]{:S(2)}) async-start(s8[4718592]{0:T(1024)(128)(4,1)} %bitcast.248), calls=%async_computation.20 | async-start | bytes 1048576
  171.2 11.7 %slice-start.2 = ((s8[4718592]{0:T(1024)(128)(4,1)}), s8[4194304]{0:T(1024)(128)(4,1)S(1)}, s32[]{:S(2)}) async-start(s8[4718592]{0:T(1024)(128)(4,1)} %bitcast.250), calls=%async_computation.21 | async-start | bytes 8388608
  172.8 10.1 %copy-start.6 = (bf16[128,4,768]{2,0,1:T(8,128)(2,1)}, bf16[128,4,768]{2,0,1:T(8,128)(2,1)S(1)}, u32[]{:S(2)}) copy-start(bf16[128,4,768]{2,0,1:T(8,128)(2,1)S(1)} %get-tuple-element.197) | copy-start | bytes 2359300
  172.8 10.1 %copy-start.11 = (f32[768]{0:T(1024)S(1)}, f32[768]{0:T(1024)}, u32[]{:S(2)}) copy-start(f32[768]{0:T(1024)} %copy-done.10) | copy-start | bytes 9220
  172.8 10.1 %slice-start.3 = ((s8[4718592]{0:T(1024)(128)(4,1)}), s8[524288]{0:T(1024)(128)(4,1)S(1)}, s32[]{:S(2)}) async-start(s8[4718592]{0:T(1024)(128)(4,1)} %bitcast.250), calls=%async_computation.22 | async-start | bytes 1048576
  182.9 4.9 copy-start.24
  188.4 1.1 copy-start.4
  188.4 1.3 copy-start.15
  189.7 0.9 copy-start.3
  192.9 213.9 %reduce-scatter.20.cloned.1.call-start = ((), (), s32[]{:S(2)}) async-start(), calls=%async_computation.13 | async-start | bytes 10616832 | tf_op jit(solution)/shard_map/reduce_scatter | solution.py:182
  217.4 6.4 copy-start.12
  219.5 24.3 %all-to-all-start.2 = ((bf16[4,128,768]{1,0,2:T(4,128)(2,1)}), bf16[4,128,768]{1,0,2:T(4,128)(2,1)}, u32[]{:S(2)}, u32[]{:S(2)}) async-start(bf16[4,128,768]{1,0,2:T(4,128)(2,1)} %copy.153), calls=%async_computation.2 | async-start | bytes 1572864 | tf_op jit(solution)/shard_map/all_to_all | solution.py:159
  223.8 185.4 %reduce-scatter.18.cloned.1.call-start = ((), (), s32[]{:S(2)}) async-start(), calls=%async_computation.12 | async-start | bytes 10616832 | tf_op jit(solution)/shard_map/reduce_scatter | solution.py:180
  233.4 12.8 %copy-start.22 = (s32[4]{0:T(128)S(1)}, s32[4]{0:T(128)}, u32[]{:S(2)}) copy-start(s32[4]{0:T(128)} %param.19) | copy-start | bytes 52
  233.4 231.4 %reduce-scatter.22.cloned.1.call-start = ((), (), s32[]{:S(2)}) async-start(), calls=%async_computation.14 | async-start | bytes 7962624
  395.7 0.7 copy-start.9
  395.7 1.3 copy-start.8
  395.7 105.9 %reduce-scatter.28.cloned.1.call-start = ((), (), s32[]{:S(2)}) async-start(), calls=%async_computation.17 | async-start | bytes 442368
  399.9 139.1 %reduce-scatter.26.cloned.1.call-start = ((), (), s32[]{:S(2)}) async-start(), calls=%async_computation.16 | async-start | bytes 442368
  401.6 174.3 %reduce-scatter.24.cloned.1.call-start = ((), (), s32[]{:S(2)}) async-start(), calls=%async_computation.15 | async-start | bytes 442368
  405.0 256.3 %all-reduce.8.cloned.1.call-start = ((), (), s32[]{:S(2)}) async-start(), calls=%async_computation.18 | async-start | bytes 3833856 | tf_op jit(solution)/shard_map/psum | solution.py:187
  467.0 2.1 copy-start.23
  469.1 70.7 %copy-start.16 = (f32[128,4]{0,1:T(4,128)S(1)}, f32[128,4]{0,1:T(4,128)}, u32[]{:S(2)}) copy-start(f32[128,4]{0,1:T(4,128)} %copy-done.15) | copy-start | bytes 6148
  663.6 3.9 copy-start.7
Sparse Core Ops, SparseCore 0:
  193.0 41.5 reduce-scatter.15
  238.5 76.4 reduce-scatter.19
  318.9 76.4 reduce-scatter.17
  399.3 65.4 reduce-scatter.21
  467.7 33.8 reduce-scatter.27
  505.1 33.8 reduce-scatter.25
  542.0 33.8 reduce-scatter.23
  579.6 81.6 all-reduce.7
where the time goes:
time: 683 us; the launch traced here: 676 us
  waiting for transfers between devices  271 us (40%)
  local copies, waits for them, and re-layouts  113 us (17%)
  blocking collectives  112 us (16%)
  matrix products  97.2 us (14%)
  other arithmetic  51.4 us (8%)
  between operations  16 us (2%)
  starting transfers between devices  15.3 us (2%)
    unnamed x12, waiting for transfers between devices  120 us
    all_to_all x1, blocking collectives, on_device(): lax.all_to_all(grad_stack, 'head', split_axis=2, concat_axis=3, tiled=True)  75.6 us
    psum x1, waiting for transfers between devices, on_device(): lax.psum(shares[0].astype(jnp.bfloat16), 'head').astype(jnp.float32)  64.8 us
    all_to_all x1, waiting for transfers between devices, on_device(): lax.all_to_all(projected, 'head', split_axis=3, concat_axis=2, tiled=True)  53.9 us
    unnamed x77, local copies, waits for them, and re-layouts  41.9 us
    unnamed x1, blocking collectives  23.7 us
    all_to_all x1, waiting for transfers between devices, on_device(): lax.all_to_all(context, 'head', split_axis=1, concat_axis=2, tiled=True)  21.2 us
  transfers between devices with their start and end apart: 11, of which 8 were waited for; matrix products, arithmetic and copies ran while one was open for 23% of the time, Pallas kernels for 0%

commit v1 on v0

v1 whole, which is shorter than its diff:
```python
import functools
import jax
import jax.numpy as jnp
from jax import lax
from jax.experimental import pallas as pl
from jax.experimental.pallas import tpu as pltpu
from jax.sharding import PartitionSpec as P

F32, BF = jnp.float32, jnp.bfloat16
L, D, F, NP = 512, 768, 3072, 6
GC0, GC1 = 0.7978845608028654, 0.044715

def nn(a, b):
    return lax.dot_general(a, b, (((1,), (0,)), ((), ())), preferred_element_type=F32)
def nt(a, b):
    return lax.dot_general(a, b, (((1,), (1,)), ((), ())), preferred_element_type=F32)
def tn(a, b):
    return lax.dot_general(a, b, (((0,), (0,)), ((), ())), preferred_element_type=F32)

def rows_loop(n, step, f):
    def it(r, c):
        f(pl.multiple_of(r * step, step))
        return c
    lax.fori_loop(0, n // step, it, 0)

def mean(v):
    return jnp.sum(v, axis=-1, keepdims=True) * (1.0 / D)

def qkv(x_ref, qi_ref, w_ref, qvb_ref, q_ref, k_ref, v_ref, qt_ref, kt_ref, vt_ref, b0, r0, rows):
    xb = x_ref[rows, :].astype(F32)
    qi = (b0 * jnp.tanh(xb * r0)).astype(BF)
    qi_ref[rows, :] = qi
    for m, (dst, tdst) in enumerate(((q_ref, qt_ref), (k_ref, kt_ref), (v_ref, vt_ref))):
        y = nn(qi, w_ref[m])
        if m == 0:
            y = (y + qvb_ref[0:1, :].astype(F32)).astype(BF).astype(F32) * 0.125
        if m == 2:
            y = y + qvb_ref[1:2, :].astype(F32)
        for p in range(NP):
            yp = y[:, p * 128:(p + 1) * 128].astype(BF)
            dst[p, rows, :] = yp
            tdst[p, :, rows] = yp.T

def attn_fwd(q_t, k_ref, v_t, p_ref, ctxt_ref, length):
    live = lax.broadcasted_iota(jnp.int32, (L, L), 0) < length
    low = lax.broadcasted_iota(jnp.int32, (128, L), 0) < 64
    def pair(p, c):
        kp = k_ref[p]
        qt = q_t[p]
        vt = v_t[p]
        for t in range(2):
            qm = jnp.where(low if t == 0 else ~low, qt, jnp.zeros_like(qt))
            s = nn(kp, qm)
            s = jnp.where(live, s, -1e9)
            e = jnp.exp(s - jnp.max(s, axis=0, keepdims=True))
            pr = (e * (1.0 / jnp.sum(e, axis=0, keepdims=True))).astype(BF)
            p_ref[2 * p + t] = pr
            ctxt_ref[p, 64 * t:64 * t + 64, :] = nn(vt[64 * t:64 * t + 64, :], pr).astype(BF)
        return c
    lax.fori_loop(0, NP, pair, 0)

def out_proj(ctxt_ref, x_ref, wo_ref, ob_ref, nv_ref, qct_ref, slc_ref, n1_ref, r1_ref, hid_ref, slh_ref, qh_ref, b1, i1, b2, i2):
    for p in range(NP):
        ct = ctxt_ref[p].astype(F32)
        th = jnp.tanh(ct * i1)
        qct_ref[p * 128:(p + 1) * 128, :] = (b1 * th).astype(BF)
        slc_ref[:, p * 128:(p + 1) * 128] = (1.0 - th * th).T
    g1, s1 = nv_ref[0:1, :].astype(F32), nv_ref[2:3, :].astype(F32)
    ob = ob_ref[...].astype(F32)
    hid_ref[...] = tn(qct_ref[...], wo_ref[...])
    def f(r):
        rows = pl.ds(r, 64)
        v = hid_ref[rows, :] + ob + x_ref[rows, :].astype(F32)
        c = v - mean(v)
        rr = lax.rsqrt(mean(c * c) + 1e-5)
        n = c * rr
        n1_ref[rows, :] = n
        r1_ref[rows, :] = jnp.broadcast_to(rr, (64, 128))
        h = n * g1 + s1
        hid_ref[rows, :] = h
        th = jnp.tanh(h * i2)
        qh_ref[rows, :] = (b2 * th).astype(BF)
        slh_ref[rows, :] = 1.0 - th * th
    rows_loop(L, 64, f)

def ffn_fwd(qh_ref, win_ref, wout_ref, fib_ref, act_ref, dfac_ref, acc_ref, b3, i3):
    acc_ref[...] = jnp.zeros_like(acc_ref)
    RB = 256
    def chunk(c, _):
        bias = fib_ref[c].astype(F32)
        for r in range(0, L, RB):
            rows = slice(r, r + RB)
            t = nn(qh_ref[rows, :], win_ref[c]) + bias
            t2 = t * t
            th = jnp.tanh(t * (GC0 + (GC0 * GC1) * t2))
            hp = 0.5 + 0.5 * th
            u = t * hp
            cl = jnp.tanh(u * i3)
            act = (b3 * cl).astype(BF)
            d = hp + u * (1.0 - th) * (GC0 + (3 * GC0 * GC1) * t2)
            act_ref[c, rows, :] = act
            dfac_ref[c, rows, :] = (d * (1.0 - cl * cl)).astype(BF)
            acc_ref[rows, :] += nn(act, wout_ref[c])
        return _
    lax.fori_loop(0, 4, chunk, 0)

def colsum_acc(vec_ref, row, val):
    vec_ref[row:row + 1, :] += jnp.sum(val, axis=0, keepdims=True)

def ln2(acc_ref, hid_ref, ct_ref, fob_ref, nv_ref, out_ref, gs_ref, gb_ref, gbt, vec_ref):
    g2, s2 = nv_ref[1:2, :].astype(F32), nv_ref[3:4, :].astype(F32)
    fob = fob_ref[...].astype(F32)
    def f(r):
        rows = pl.ds(r, 64)
        v = acc_ref[rows, :] + fob + hid_ref[rows, :]
        c = v - mean(v)
        rr = lax.rsqrt(mean(c * c) + 1e-5)
        n = c * rr
        out_ref[rows, :] = (n * g2 + s2).astype(BF)
        ct = ct_ref[rows, :].astype(F32)
        cn = ct * n
        colsum_acc(vec_ref, 4, cn)
        colsum_acc(vec_ref, 6, ct)
        q = ct * g2
        gs = rr * (q - mean(q) - n * mean(q * n))
        gs_ref[rows, :] = gs
        gb = gs.astype(BF)
        gb_ref[rows, :] = gb
        colsum_acc(vec_ref, 7, gb.astype(F32))
    rows_loop(L, 64, f)

def ffn_bwd(gb_ref, qh_ref, win_ref, wout_ref, act_ref, dfac_ref, acc_ref, qht_ref, gfo, gfi, vec_ref):
    for p in range(NP):
        qht_ref[p * 128:(p + 1) * 128, :] = qh_ref[:, p * 128:(p + 1) * 128].T
    acc_ref[...] = jnp.zeros_like(acc_ref)
    def chunk(c, _):
        gfo(c, tn(act_ref[c], gb_ref[...]))
        return _
    lax.fori_loop(0, 4, chunk, 0)
    def chunk2(c, _):
        for r in range(0, L, 256):
            rows = slice(r, r + 256)
            ga = nt(gb_ref[rows, :], wout_ref[c])
            gp = (ga * dfac_ref[c, rows, :].astype(F32)).astype(BF)
            dfac_ref[c, rows, :] = gp
            vec_ref[pl.ds(8 + c, 1), :] += jnp.sum(gp.astype(F32), axis=0, keepdims=True)
            acc_ref[rows, :] += nt(gp, win_ref[c])
        gfi(c, nn(qht_ref[...], dfac_ref[c]))
        return _
    lax.fori_loop(0, 4, chunk2, 0)

def ln1_bwd(acc_ref, gs_ref, slh_ref, n1_ref, r1_ref, nv_ref, gat_ref, vec_ref):
    g1 = nv_ref[0:1, :].astype(F32)
    def f(r):
        rows = pl.ds(r, 64)
        gh = gs_ref[rows, :] + acc_ref[rows, :] * slh_ref[rows, :]
        n = n1_ref[rows, :]
        colsum_acc(vec_ref, 3, gh * n)
        colsum_acc(vec_ref, 5, gh)
        q = gh * g1
        gs = r1_ref[rows, 0:1] * (q - mean(q) - n * mean(q * n))
        gs_ref[rows, :] = gs
        gat = gs.astype(BF)
        gat_ref[rows, :] = gat
        colsum_acc(vec_ref, 2, gat.astype(F32))
    rows_loop(L, 64, f)

def out_bwd(gat_ref, wo_ref, qct_ref, slc_ref, dc_ref, dct_ref, go):
    go(nn(qct_ref[...], gat_ref[...]))
    g = nt(gat_ref[...], wo_ref[...])
    for p in range(NP):
        cols = slice(p * 128, (p + 1) * 128)
        d = (g[:, cols] * slc_ref[:, cols]).astype(BF)
        dc_ref[p] = d
        dct_ref[p] = d.T

def attn_bwd(q_ref, k_t, v_ref, dc_ref, dc_t, p_ref, dq_ref, dk_ref, dv_ref):
    low = lax.broadcasted_iota(jnp.int32, (128, L), 0) < 64
    lane_low = lax.broadcasted_iota(jnp.int32, (L, 128), 1) < 64
    def pair(p, c):
        qp, kt, vp, dc, dct = q_ref[p], k_t[p], v_ref[p], dc_ref[p], dc_t[p]
        res = []
        for t in range(2):
            dm = jnp.where(low if t == 0 else ~low, dct, jnp.zeros_like(dct))
            dp = nn(vp, dm)
            pr = p_ref[2 * p + t]
            prf = pr.astype(F32)
            delta = jnp.sum(dp * prf, axis=0, keepdims=True)
            ds = (prf * (dp - delta)).astype(BF)
            dv = nn(pr, dc)
            dk = nn(ds, qp)
            dqt = nn(kt[64 * t:64 * t + 64, :], ds) * 0.125
            res.append((dv, dk, dqt))
        dv_ref[p] = jnp.where(lane_low, res[0][0], res[1][0]).astype(BF)
        dk_ref[p] = jnp.where(lane_low, res[0][1], res[1][1]).astype(BF)
        dq_ref[p] = jnp.concatenate([res[0][2], res[1][2]], axis=0).astype(BF).T
        return c
    lax.fori_loop(0, NP, pair, 0)

def qkv_bwd(qi_ref, qit_ref, x_ref, w_ref, dq_ref, dk_ref, dv_ref, gs_ref, acc_ref, gq, gx_ref, vec_ref, b0, i0):
    for p in range(NP):
        qit_ref[p * 128:(p + 1) * 128, :] = qi_ref[:, p * 128:(p + 1) * 128].T
    for m, ref in enumerate((dq_ref, dk_ref, dv_ref)):
        d = jnp.concatenate([ref[p] for p in range(NP)], axis=1)
        gq(m, nn(qit_ref[...], d))
        if m != 1:
            colsum_acc(vec_ref, 0 if m == 0 else 1, d.astype(F32))
        if m == 0:
            acc_ref[...] = nt(d, w_ref[m])
        else:
            acc_ref[...] += nt(d, w_ref[m])
    def f(r):
        rows = pl.ds(r, 64)
        th = jnp.tanh(x_ref[rows, :].astype(F32) * i0)
        gx_ref[rows, :] = (gs_ref[rows, :] + acc_ref[rows, :] * (1.0 - th * th)).astype(BF)
    rows_loop(L, 64, f)


class LaneSlots:
    def __init__(self, ref):
        self.ref = ref

    def __getitem__(self, p):
        return self.ref[0, :, pl.ds(pl.multiple_of(p * 128, 128), 128)]

    def __setitem__(self, p, value):
        self.ref[0, :, pl.ds(pl.multiple_of(p * 128, 128), 128)] = value


def kernel(x_ref, len_ref, rng_ref, wqkv_ref, qvb_ref, wo_ref, ob_ref, nv_ref, win_ref, fib_ref, wout_ref, fob_ref, ct_ref,
           out_ref, gx_ref, g_ref, vec_ref,
           qi_ref, q_ref, k_ref, v_ref, qt_ref, kt_ref, vt_ref, p_ref, ctxt_ref, qct_ref, slc_ref, n1_ref, r1_ref, hid_ref, slh_ref,
           qh_ref, act_ref, dfac_ref, acc_ref, gs_ref, gb_ref):
    b = [jnp.full((1, 1), rng_ref[i], jnp.int32).astype(F32) * (1 / 16.0) for i in range(4)]
    iv = [1.0 / t for t in b]
    vec_ref[...] = jnp.zeros_like(vec_ref)
    for r in range(0, L, 256):
        qkv(x_ref, qi_ref, wqkv_ref, qvb_ref, q_ref, k_ref, v_ref, qt_ref, kt_ref, vt_ref, b[0], iv[0], slice(r, r + 256))
    attn_fwd(qt_ref, k_ref, vt_ref, p_ref, ctxt_ref, len_ref[0])
    out_proj(ctxt_ref, x_ref, wo_ref, ob_ref, nv_ref, qct_ref, slc_ref, n1_ref, r1_ref, hid_ref, slh_ref, qh_ref, b[1], iv[1], b[2], iv[2])
    ffn_fwd(qh_ref, win_ref, wout_ref, fib_ref, act_ref, dfac_ref, acc_ref, b[3], iv[3])
    ln2(acc_ref, hid_ref, ct_ref, fob_ref, nv_ref, out_ref, gs_ref, gb_ref, None, vec_ref)

    def put(i):
        def f(c, v):
            g_ref[i + c] = v.astype(BF)
        return f

    ffn_bwd(gb_ref, qh_ref, win_ref, wout_ref, act_ref, dfac_ref, acc_ref, vt_ref.reshape(D, L), put(4), put(0), vec_ref)
    ln1_bwd(acc_ref, gs_ref, slh_ref, n1_ref, r1_ref, nv_ref, gb_ref, vec_ref)
    dc = LaneSlots(act_ref)
    out_bwd(gb_ref, wo_ref, qct_ref, slc_ref, dc, vt_ref, functools.partial(put(8), 0))
    attn_bwd(q_ref, kt_ref, v_ref, dc, vt_ref, p_ref, q_ref, k_ref, v_ref)
    qkv_bwd(qi_ref, qct_ref, x_ref, wqkv_ref, q_ref, k_ref, v_ref, gs_ref, acc_ref, put(9), gx_ref, vec_ref, b[0], iv[0])


def layer(*args):
    def vm(*s, d=BF):
        return pltpu.VMEM(s, d)
    scratch = [vm(L, D), vm(6, L, 128), vm(6, L, 128), vm(6, L, 128), vm(6, 128, L), vm(6, 128, L), vm(6, 128, L), vm(12, L, L),
               vm(6, 128, L), vm(D, L), vm(L, D, d=F32), vm(L, D, d=F32), vm(L, 128, d=F32), vm(L, D, d=F32), vm(L, D, d=F32),
               vm(L, D), vm(4, L, D), vm(4, L, D), vm(L, D, d=F32), vm(L, D, d=F32), vm(L, D)]
    outs = [jax.ShapeDtypeStruct((L, D), BF), jax.ShapeDtypeStruct((L, D), BF), jax.ShapeDtypeStruct((12, D, D), BF),
            jax.ShapeDtypeStruct((16, D), F32)]
    v, s = pl.BlockSpec(memory_space=pltpu.VMEM), pl.BlockSpec(memory_space=pltpu.SMEM)
    return pl.pallas_call(
        kernel, out_shape=outs, in_specs=[v, s, s] + [v] * 10, out_specs=[v] * 4, scratch_shapes=scratch,
        compiler_params=pltpu.CompilerParams(vmem_limit_bytes=64 * 1024 * 1024 - 65536))(*args)


def on_device(n_dp, tokens, lengths, ranges, qkv_weight, qv_bias, out_weight, out_bias, norm_gains, norm_shifts, ffn_in, ffn_in_bias,
              ffn_out, ffn_out_bias, cotangent):
    def to_seq(a):
        return lax.all_to_all(a.transpose(1, 0, 2), "head", split_axis=0, concat_axis=1, tiled=True)[0]

    def to_pos(a):
        return lax.all_to_all(a[None], "head", split_axis=1, concat_axis=0, tiled=True).transpose(1, 0, 2)

    length = lax.dynamic_slice(lengths, (lax.axis_index("head"),), (1,))
    out, gx, g, vec = layer(
        to_seq(tokens), length, ranges, qkv_weight, qv_bias, out_weight, out_bias[None], jnp.concatenate([norm_gains, norm_shifts]),
        ffn_in.reshape(D, 4, D).transpose(1, 0, 2), ffn_in_bias.reshape(4, 1, D), ffn_out.reshape(4, D, D), ffn_out_bias[None],
        to_seq(cotangent))
    rs = D // n_dp
    wout = lax.psum_scatter(g[4:8].reshape(4 * D, D), "dp", scatter_dimension=0, tiled=True)
    rest = lax.psum_scatter(jnp.concatenate([g[0:4], g[8:12]]), "dp", scatter_dimension=1, tiled=True)
    both = lax.psum(jnp.concatenate([wout, rest.reshape(8 * rs, D)]), "head").astype(F32)
    wout, rest = both[:4 * rs], both[4 * rs:].reshape(8, rs, D)
    vec = lax.psum(vec, ("dp", "head"))
    i = lax.axis_index("dp")

    def mine(v):
        return lax.dynamic_slice_in_dim(v, i * rs, rs, axis=-1)
    fib = lax.dynamic_slice(vec[8:12].reshape(-1), (i * 4 * rs,), (4 * rs,))
    return (to_pos(out), to_pos(gx).astype(F32), rest[5:8], mine(vec[0:2]), rest[4], mine(vec[2]), mine(vec[3:5]), mine(vec[5:7]),
            rest[0:4].transpose(1, 0, 2).reshape(rs, F), fib, wout, mine(vec[7]))


def solution(mesh):
    tok = P("head", "dp", None)
    return jax.shard_map(
        functools.partial(on_device, mesh.shape["dp"]),
        mesh=mesh,
        in_specs=(tok, P("dp")) + (P(),) * 11 + (tok,),
        out_specs=(tok, tok, P(None, "dp", None), P(None, "dp"), P("dp", None), P("dp"), P(None, "dp"), P(None, "dp"),
                   P("dp", None), P("dp"), P("dp", None), P("dp")),
        check_vma=False,
    )
```

time: 683 us -> 378 us (0.55); the launches traced: 676 us -> 377 us
  waiting for transfers between devices: 271 us -> 146 us
  matrix products: 97.2 us -> 0 us
  Pallas kernels: 0 us -> 65.6 us
  local copies, waits for them, and re-layouts: 113 us -> 49.2 us
  blocking collectives: 112 us -> 59.9 us
  other arithmetic: 51.4 us -> 23.6 us
    unnamed x12 -> x3, waiting for transfers between devices: 120 us -> 0.05 us
    reduce_scatter x3 -> x2, waiting for transfers between devices: 0.02 us -> 111 us  [the longest x1 80.4 us: on_device(): lax.psum_scatter(jnp.concatenate([g[0:4], g[8:12]]), 'dp', scatter_dimens...]
    dot_general x40 -> x0, matrix products: 97.2 us -> none  [the longest x1 11.7 us: on_device(): jnp.einsum('psf,psd->fd', act, grad_branch, preferred_element_type=jnp.fl...]
    all_to_all x1 -> x0, blocking collectives: 75.6 us -> none  [on_device(): lax.all_to_all(grad_stack, 'head', split_axis=2, concat_axis=3, tiled=True)]
    pallas_call x0 -> x1, Pallas kernels: none -> 65.6 us  [layer(): pl.pallas_call(kernel, out_shape=outs, in_specs=[v, s, s] + [v] * 10, out...]
    all_to_all x3 -> x4, waiting for transfers between devices: 85.5 us -> 22.4 us  [the longest x2 22.4 us: to_seq(): lax.all_to_all(a.transpose(1, 0, 2), 'head', split_axis=0, concat_axis=1,...]
    psum x1, waiting for transfers between devices: 64.8 us -> 12.7 us  [on_device(): lax.psum(jnp.concatenate([wout, rest.reshape(8 * rs, D)]), 'head')]
    psum x1, blocking collectives: 12.5 us -> 59.9 us  [on_device(): vec = lax.psum(vec, ('dp', 'head'))]
  transfers between devices with their start and end apart: 11 -> 7, of which waited for: 8 -> 5; matrix products, arithmetic and copies ran while one was open for 23% -> 14% of each run, Pallas kernels for 0% -> 0%
where the time goes in v1:
time: 378 us; the launch traced here: 377 us
  waiting for transfers between devices  146 us (39%)
  Pallas kernels  65.6 us (17%)
  blocking collectives  59.9 us (16%)
  local copies, waits for them, and re-layouts  49.2 us (13%)
  other arithmetic  23.6 us (6%)
  starting transfers between devices  19.1 us (5%)
  between operations  13.9 us (4%)
    reduce_scatter x1, waiting for transfers between devices, on_device(): lax.psum_scatter(jnp.concatenate([g[0:4], g[8:12]]), 'dp', scatter_dimens...  80.4 us
    pallas_call x1, Pallas kernels, layer(): pl.pallas_call(kernel, out_shape=outs, in_specs=[v, s, s] + [v] * 10, out...  65.6 us
    psum x1, blocking collectives, on_device(): vec = lax.psum(vec, ('dp', 'head'))  59.9 us
    reduce_scatter x1, waiting for transfers between devices, on_device(): lax.psum_scatter(g[4:8].reshape(4 * D, D), 'dp', scatter_dimension=0, til...  30.4 us
    all_to_all x2, waiting for transfers between devices, to_seq(): lax.all_to_all(a.transpose(1, 0, 2), 'head', split_axis=0, concat_axis=1,...  22.4 us
    unnamed x35, local copies, waits for them, and re-layouts  16.7 us
    psum x1, waiting for transfers between devices, on_device(): lax.psum(jnp.concatenate([wout, rest.reshape(8 * rs, D)]), 'head')  12.7 us
    slice x1, local copies, waits for them, and re-layouts, on_device(): g[4:8].reshape(4 * D, D)  11 us
  transfers between devices with their start and end apart: 7, of which 5 were waited for; matrix products, arithmetic and copies ran while one was open for 14% of the time, Pallas kernels for 0%

profile of v1, /device:TPU:0, one launch (start us, length us, event | category | flops | bytes accessed | tf_op | source)
XLA Modules:
  0.0 377.5 jit_solution(2455928143366034092)
XLA Ops:
  7.2 2.2 copy.69
  9.4 6.3 %all-to-all-start = ((bf16[4,128,768]{2,1,0:T(8,128)(2,1)}), bf16[4,128,768]{2,1,0:T(8,128)(2,1)S(1)}, u32[]{:S(2)}, u32[]{:S(2)}) async-start(bf16[4,128,768]{2,1,0:T(8,128)(2,1)} %bitcast.37), calls=%async_computation | async-start | bytes 1572864 | tf_op jit(solution)/shard_map/all_to_all | solution.py:274
  15.7 1.0 copy.68
  16.6 19.1 %all-to-all-done = bf16[4,128,768]{2,1,0:T(8,128)(2,1)S(1)} async-done(((bf16[4,128,768]{2,1,0:T(8,128)(2,1)}), bf16[4,128,768]{2,1,0:T(8,128)(2,1)S(1)}, u32[]{:S(2)}, u32[]{:S(2)}) %all-to-all-start) | async-done | bytes 786464 | tf_op jit(solution)/shard_map/all_to_all | solution.py:274
  35.8 4.2 %all-to-all-start.1 = ((bf16[4,128,768]{2,1,0:T(8,128)(2,1)}), bf16[4,128,768]{2,1,0:T(8,128)(2,1)}, u32[]{:S(2)}, u32[]{:S(2)}) async-start(bf16[4,128,768]{2,1,0:T(8,128)(2,1)} %bitcast.36), calls=%async_computation.1 | async-start | bytes 1572864 | tf_op jit(solution)/shard_map/all_to_all | solution.py:274
  40.0 0.0 reduce-scatter.3.cloned.1.call-start
  40.0 6.6 %copy.50 = bf16[768,3072]{0,1:T(8,128)(2,1)} copy(bf16[768,3072]{1,0:T(8,128)(2,1)} %param.23) | data formatting | bytes 9437184 | tf_op args[9]
  46.7 6.7 %copy.51 = bf16[768,4,768]{2,0,1:T(8,128)(2,1)} copy(bf16[768,4,768]{0,2,1:T(8,128)(2,1)} %bitcast.42) | data formatting | bytes 9437184 | tf_op jit(solution)/shard_map/reshape | solution.py:282
  53.4 0.6 reshape.76.fib_ref
  54.0 0.6 broadcast_in_dim.12.ob_ref
  54.6 0.6 broadcast_in_dim.13.fob_ref
  55.2 0.6 dynamic_slice.25.len_ref
  55.8 0.6 pad_maximum_fusion.2.nv_ref
  56.4 3.2 all-to-all-done.1
  59.7 65.6 %shard_map.229 = (bf16[512,768]{1,0:T(8,128)(2,1)}, bf16[512,768]{1,0:T(8,128)(2,1)}, bf16[12,768,768]{2,1,0:T(8,128)(2,1)}, f32[16,768]{1,0:T(8,128)}) custom-call(bf16[512,768]{1,0:T(8,128)(2,1)} %bitcast.50, s32[1]{0:T(128)} %dynamic_slice.25.len_ref, s32[4]{0:T(128)} %rng_ref.1, bf16[3,768,768]{2,1,0:T(8,128)(2,1)} %wqkv_ref.1, bf16[2,768]{1,0:T(2,128)(2,1)} %qvb_ref.1, ...), custom_call_target="tpu_custom_call" | custom-call | tf_op jit(solution)/shard_map/pallas_call | solution.py:266
  125.3 11.0 %fusion.2 = (bf16[4,768,768]{2,1,0:T(8,128)(2,1)}, bf16[4,768,768]{2,1,0:T(8,128)(2,1)}, bf16[4,768,768]{2,1,0:T(8,128)(2,1)}) fusion(bf16[12,768,768]{2,1,0:T(8,128)(2,1)} %get-tuple-element.18), kind=kLoop, calls=%fused_computation.13 | loop fusion | bytes 28311552 | tf_op jit(solution)/shard_map/slice | solution.py:285
  136.3 0.0 reduce-scatter.5.cloned.1.call-start
  136.3 9.4 %pad_maximum_fusion = bf16[8,768,768]{2,1,0:T(8,128)(2,1)} fusion(bf16[4,768,768]{2,1,0:T(8,128)(2,1)} %get-tuple-element.33, bf16[4,768,768]{2,1,0:T(8,128)(2,1)} %get-tuple-element.34), kind=kLoop, calls=%fused_computation | loop fusion | flops 4718592 | bytes 18874368 | tf_op jit(solution)/shard_map/concatenate | solution.py:286
  145.7 1.2 copy-done.4
  147.0 1.2 copy.70
  148.2 0.5 broadcast
  148.7 5.4 %reduce.1 = bf16[512,768]{1,0:T(8,128)(2,1)S(1)} reduce(bf16[512,1,768]{2,1,0:T(2,128)(2,1)S(1)} %bitcast.43, bf16[]{:T(256)} %broadcast), dimensions={1}, to_apply=%bitcast.38.reduce_sub_computation | reduce | bytes 1572866
  154.1 1.0 reshape.77
  155.1 3.6 all-to-all-start.3
  158.8 0.3 all-reduce.2.cloned.1.call-start
  159.0 30.4 %reduce-scatter.3.cloned.1.call-done = bf16[384,768]{1,0:T(8,128)(2,1)} async-done(((bf16[3072,768]{1,0:T(8,128)(2,1)}), bf16[384,768]{1,0:T(8,128)(2,1)}) %reduce-scatter.3.cloned.1.call-update) | async-done | bytes 589840 | tf_op jit(solution)/shard_map/reduce_scatter | solution.py:285
  189.4 80.4 %reduce-scatter.5.cloned.1.call-done = bf16[8,96,768]{2,1,0:T(8,128)(2,1)} async-done(((bf16[8,768,768]{2,1,0:T(8,128)(2,1)}), bf16[8,96,768]{2,1,0:T(8,128)(2,1)}) %reduce-scatter.5.cloned.1.call-update) | async-done | bytes 1179664 | tf_op jit(solution)/shard_map/reduce_scatter | solution.py:286
  269.8 2.8 pad_maximum_fusion.1
  272.7 1.2 copy.71
  273.9 5.4 %reduce = bf16[512,768]{1,0:T(8,128)(2,1)S(1)} reduce(bf16[512,1,768]{2,1,0:T(2,128)(2,1)S(1)} %bitcast.44, bf16[]{:T(256)} %broadcast), dimensions={1}, to_apply=%bitcast.39.reduce_sub_computation | reduce | bytes 1572866
  279.3 1.0 reshape.79
  280.3 4.6 %all-to-all-start.2 = ((bf16[4,2,49152]{2,1,0:T(2,128)(2,1)}), bf16[4,2,49152]{2,1,0:T(2,128)(2,1)S(1)}, u32[]{:S(2)}, u32[]{:S(2)}) async-start(bf16[4,2,49152]{2,1,0:T(2,128)(2,1)} %reshape.79), calls=%async_computation.2 | async-start | bytes 1572864 | tf_op jit(solution)/shard_map/all_to_all | solution.py:277
  284.9 59.9 %psum.15 = f32[16,768]{1,0:T(8,128)S(1)} all-reduce(f32[16,768]{1,0:T(8,128)S(1)} %copy-done.5), channel_id=1, replica_groups=mesh['dp'=8,'head'=4] {'dp','head'}, use_global_device_ids=true, to_apply=%region_3.0 | all-reduce | flops 12288 | bytes 98304 | tf_op jit(solution)/shard_map/psum | solution.py:289
  344.9 0.7 dynamic_slice.31
  345.6 0.6 constant_dynamic-slice_fusion.4
  346.2 0.6 fusion
  346.8 0.6 constant_dynamic-slice_fusion.1
  347.4 0.7 reshape.78
  348.2 0.1 copy.60
  348.3 2.2 copy.67
  350.5 0.7 reshape.80
  351.2 0.1 copy.59
  351.3 1.5 copy.58
  352.8 12.7 %all-reduce.2.cloned.1.call-done = bf16[1152,768]{1,0:T(8,128)(2,1)} async-done(((bf16[1152,768]{1,0:T(8,128)(2,1)}), bf16[1152,768]{1,0:T(8,128)(2,1)}) %all-reduce.2.cloned.1.call-update) | async-done | bytes 1769488 | tf_op jit(solution)/shard_map/psum | solution.py:287
  365.6 2.5 fusion.3
  368.1 1.1 copy.61
  369.2 1.0 slice.65
  370.2 0.7 slice.67
  (32 shorter events, 0.1 us)
Async XLA Ops:
  7.2 8.5 %copy-start.2 = (bf16[128,4,768]{2,1,0:T(4,128)(2,1)S(1)}, bf16[128,4,768]{2,1,0:T(4,128)(2,1)}, u32[]{:S(2)}) copy-start(bf16[128,4,768]{2,1,0:T(4,128)(2,1)} %param.27) | copy-start | bytes 2359300
  9.4 26.4 %all-to-all-start = ((bf16[4,128,768]{2,1,0:T(8,128)(2,1)}), bf16[4,128,768]{2,1,0:T(8,128)(2,1)S(1)}, u32[]{:S(2)}, u32[]{:S(2)}) async-start(bf16[4,128,768]{2,1,0:T(8,128)(2,1)} %bitcast.37), calls=%async_computation | async-start | bytes 1572864 | tf_op jit(solution)/shard_map/all_to_all | solution.py:274
  35.8 10.9 %copy-start.1 = (bf16[4,128,768]{2,1,0:T(8,128)(2,1)}, bf16[4,128,768]{2,1,0:T(8,128)(2,1)S(1)}, u32[]{:S(2)}) copy-start(bf16[4,128,768]{2,1,0:T(8,128)(2,1)S(1)} %all-to-all-done) | copy-start | bytes 2359300
  35.8 23.9 %all-to-all-start.1 = ((bf16[4,128,768]{2,1,0:T(8,128)(2,1)}), bf16[4,128,768]{2,1,0:T(8,128)(2,1)}, u32[]{:S(2)}, u32[]{:S(2)}) async-start(bf16[4,128,768]{2,1,0:T(8,128)(2,1)} %bitcast.36), calls=%async_computation.1 | async-start | bytes 1572864 | tf_op jit(solution)/shard_map/all_to_all | solution.py:274
  40.0 149.5 %reduce-scatter.3.cloned.1.call-start = ((), (), s32[]{:S(2)}) async-start(), calls=%async_computation.6 | async-start | bytes 5308416 | tf_op jit(solution)/shard_map/reduce_scatter | solution.py:285
  46.7 6.8 %copy-start.6 = (bf16[3072]{0:T(1024)(128)(2,1)S(1)}, bf16[3072]{0:T(1024)(128)(2,1)}, u32[]{:S(2)}) copy-start(bf16[3072]{0:T(1024)(128)(2,1)} %param.24) | copy-start | bytes 18436
  46.7 7.4 %copy-start.9 = (bf16[768]{0:T(1024)(128)(2,1)S(1)}, bf16[768]{0:T(1024)(128)(2,1)}, u32[]{:S(2)}) copy-start(bf16[768]{0:T(1024)(128)(2,1)} %param.20) | copy-start | bytes 4612
  46.7 8.0 %copy-start.10 = (bf16[768]{0:T(1024)(128)(2,1)S(1)}, bf16[768]{0:T(1024)(128)(2,1)}, u32[]{:S(2)}) copy-start(bf16[768]{0:T(1024)(128)(2,1)} %param.26) | copy-start | bytes 4612
  46.7 8.5 %copy-start.11 = (s32[4]{0:T(128)S(1)}, s32[4]{0:T(128)}, u32[]{:S(2)}) copy-start(s32[4]{0:T(128)} %param.15) | copy-start | bytes 52
  46.7 9.1 %copy-start.7 = (bf16[2,768]{1,0:T(2,128)(2,1)S(1)}, bf16[2,768]{1,0:T(2,128)(2,1)}, u32[]{:S(2)}) copy-start(bf16[2,768]{1,0:T(2,128)(2,1)} %param.22) | copy-start | bytes 9220
  46.7 9.1 %copy-start.8 = (bf16[2,768]{1,0:T(2,128)(2,1)S(1)}, bf16[2,768]{1,0:T(2,128)(2,1)}, u32[]{:S(2)}) copy-start(bf16[2,768]{1,0:T(2,128)(2,1)} %param.21) | copy-start | bytes 9220
  136.3 133.6 %reduce-scatter.5.cloned.1.call-start = ((), (), s32[]{:S(2)}) async-start(), calls=%async_computation.7 | async-start | bytes 10616832 | tf_op jit(solution)/shard_map/reduce_scatter | solution.py:286
  145.7 1.2 copy-start.4
  155.1 117.5 %copy-start.3 = (bf16[512,768]{1,0:T(8,128)(2,1)S(1)}, bf16[512,768]{1,0:T(8,128)(2,1)}, u32[]{:S(2)}) copy-start(bf16[512,768]{1,0:T(8,128)(2,1)} %get-tuple-element.16) | copy-start | bytes 2359300
  155.1 125.2 %all-to-all-start.3 = ((bf16[4,2,49152]{2,1,0:T(2,128)(2,1)}), bf16[4,2,49152]{2,1,0:T(2,128)(2,1)S(1)}, u32[]{:S(2)}, u32[]{:S(2)}) async-start(bf16[4,2,49152]{2,1,0:T(2,128)(2,1)} %reshape.77), calls=%async_computation.3 | async-start | bytes 1572864 | tf_op jit(solution)/shard_map/all_to_all | solution.py:277
  158.8 206.8 %all-reduce.2.cloned.1.call-start = ((), (), s32[]{:S(2)}) async-start(), calls=%async_computation.8 | async-start | bytes 3538944 | tf_op jit(solution)/shard_map/psum | solution.py:287
  272.7 12.3 %copy-start.5 = (f32[16,768]{1,0:T(8,128)S(1)}, f32[16,768]{1,0:T(8,128)}, u32[]{:S(2)}) copy-start(f32[16,768]{1,0:T(8,128)} %get-tuple-element.19) | copy-start | bytes 147460
  280.3 70.1 %all-to-all-start.2 = ((bf16[4,2,49152]{2,1,0:T(2,128)(2,1)}), bf16[4,2,49152]{2,1,0:T(2,128)(2,1)S(1)}, u32[]{:S(2)}, u32[]{:S(2)}) async-start(bf16[4,2,49152]{2,1,0:T(2,128)(2,1)} %reshape.79), calls=%async_computation.2 | async-start | bytes 1572864 | tf_op jit(solution)/shard_map/all_to_all | solution.py:277
  365.6 3.7 copy-start
Sparse Core Ops, SparseCore 0:
  136.4 52.9 reduce-scatter.2
  193.3 76.4 reduce-scatter.4
  272.8 92.7 all-reduce.1

commit v2 on v1

v2 whole, which is shorter than its diff:
```python
import functools
import jax
import jax.numpy as jnp
from jax import lax
from jax.experimental import pallas as pl
from jax.experimental.pallas import tpu as pltpu
from jax.sharding import PartitionSpec as P

F32, BF = jnp.float32, jnp.bfloat16
L, D, F, NP = 512, 768, 3072, 6
GC0, GC1 = 0.7978845608028654, 0.044715


def nn(a, b):
    return lax.dot_general(a, b, (((1,), (0,)), ((), ())), preferred_element_type=F32)


def nt(a, b):
    return lax.dot_general(a, b, (((1,), (1,)), ((), ())), preferred_element_type=F32)


def tn(a, b):
    return lax.dot_general(a, b, (((0,), (0,)), ((), ())), preferred_element_type=F32)


def rows_loop(n, step, f):
    def it(r, c):
        f(pl.multiple_of(r * step, step))
        return c
    lax.fori_loop(0, n // step, it, 0)


def mean(v):
    return jnp.sum(v, axis=-1, keepdims=True) * (1.0 / D)


class LaneSlots:
    def __init__(self, ref):
        self.ref = ref

    def __getitem__(self, p):
        return self.ref[0, :, pl.ds(pl.multiple_of(p * 128, 128), 128)]

    def __setitem__(self, p, value):
        self.ref[0, :, pl.ds(pl.multiple_of(p * 128, 128), 128)] = value


def qkv(x_ref, qi_ref, w_ref, sm, q_ref, k_ref, v_ref, qt_ref, kt_ref, vt_ref, b0, r0, rows):
    xb = x_ref[rows, :].astype(F32)
    qi = (b0 * jnp.tanh(xb * r0)).astype(BF)
    qi_ref[rows, :] = qi
    for m, (dst, tdst) in enumerate(((q_ref, qt_ref), (k_ref, kt_ref), (v_ref, vt_ref))):
        y = nn(qi, w_ref[m])
        if m == 0:
            y = (y + sm[0:1, :]).astype(BF).astype(F32) * 0.125
        if m == 2:
            y = y + sm[1:2, :]
        for p in range(NP):
            yp = y[:, p * 128:(p + 1) * 128].astype(BF)
            dst[p, rows, :] = yp
            tdst[p, :, rows] = yp.T


def attn_fwd(q_t, k_ref, v_t, p_ref, ctxt_ref, length):
    live = lax.broadcasted_iota(jnp.int32, (L, L), 0) < length
    low = lax.broadcasted_iota(jnp.int32, (128, L), 0) < 64

    def pair(p, c):
        kp, qt, vt = k_ref[p], q_t[p], v_t[p]
        for t in range(2):
            qm = jnp.where(low if t == 0 else ~low, qt, jnp.zeros_like(qt))
            s = jnp.where(live, nn(kp, qm), -1e9)
            e = jnp.exp(s - jnp.max(s, axis=0, keepdims=True))
            pr = (e * (1.0 / jnp.sum(e, axis=0, keepdims=True))).astype(BF)
            p_ref[2 * p + t] = pr
            ctxt_ref[p, 64 * t:64 * t + 64, :] = nn(vt[64 * t:64 * t + 64, :], pr).astype(BF)
        return c
    lax.fori_loop(0, NP, pair, 0)


def out_proj(ctxt_ref, x_ref, wo_ref, sm, qct_ref, slc_ref, n1_ref, r1_ref, hid_ref, slh_ref, qh_ref, acc_ref, b1, i1, b2, i2):
    for p in range(NP):
        th = jnp.tanh(ctxt_ref[p].astype(F32) * i1)
        qct_ref[p * 128:(p + 1) * 128, :] = (b1 * th).astype(BF)
        slc_ref[:, p * 128:(p + 1) * 128] = (1.0 - th * th).astype(BF).T
    hid_ref[...] = tn(qct_ref[...], wo_ref[...])

    def f(r):
        rows = pl.ds(r, 64)
        v = hid_ref[rows, :] + sm[2:3, :] + x_ref[rows, :].astype(F32)
        c = v - mean(v)
        rr = lax.rsqrt(mean(c * c) + 1e-5)
        n = c * rr
        n1_ref[rows, :] = n
        r1_ref[rows, :] = jnp.broadcast_to(rr, (64, 128))
        h = n * sm[3:4, :] + sm[5:6, :]
        hid_ref[rows, :] = h
        th = jnp.tanh(h * i2)
        qh_ref[rows, :] = (b2 * th).astype(BF)
        slh_ref[rows, :] = (1.0 - th * th).astype(BF)
    rows_loop(L, 64, f)
    acc_ref[...] = jnp.zeros_like(acc_ref)


def ffn_fwd(qh_ref, w, sm, act_ref, dfac_ref, acc_ref, b3, i3, before, after):
    def chunk(c, _):
        s = before(c)
        bias = sm[pl.ds(8 + c, 1), :]
        for r in range(0, L, 256):
            rows = slice(r, r + 256)
            t = nn(qh_ref[rows, :], w[s]) + bias
            t2 = t * t
            th = jnp.tanh(t * (GC0 + (GC0 * GC1) * t2))
            hp = 0.5 + 0.5 * th
            u = t * hp
            cl = jnp.tanh(u * i3)
            act = (b3 * cl).astype(BF)
            d = hp + u * (1.0 - th) * (GC0 + (3 * GC0 * GC1) * t2)
            act_ref[c, rows, :] = act
            dfac_ref[c, rows, :] = (d * (1.0 - cl * cl)).astype(BF)
            acc_ref[rows, :] += nn(act, w[s + 1])
        after(c)
        return _
    lax.fori_loop(0, 4, chunk, 0)


def colsum(vec, row, val):
    vec[row:row + 1, :] += jnp.sum(val, axis=0, keepdims=True)


def ln2(acc_ref, hid_ref, ct_ref, sm, gb_ref, vec):
    def f(r):
        rows = pl.ds(r, 64)
        v = acc_ref[rows, :] + sm[7:8, :] + hid_ref[rows, :]
        c = v - mean(v)
        rr = lax.rsqrt(mean(c * c) + 1e-5)
        n = c * rr
        ct = ct_ref[rows, :].astype(F32)
        ct_ref[rows, :] = (n * sm[4:5, :] + sm[6:7, :]).astype(BF)
        colsum(vec, 4, ct * n)
        colsum(vec, 6, ct)
        q = ct * sm[4:5, :]
        gs = rr * (q - mean(q) - n * mean(q * n))
        hid_ref[rows, :] = gs
        gb = gs.astype(BF)
        gb_ref[rows, :] = gb
        colsum(vec, 7, gb.astype(F32))
    rows_loop(L, 64, f)


def ffn_bwd_out(gb_ref, qh_ref, act_ref, qht_ref, put):
    for p in range(NP):
        qht_ref[p * 128:(p + 1) * 128, :] = qh_ref[:, p * 128:(p + 1) * 128].T

    def chunk(c, _):
        put(c, tn(act_ref[c], gb_ref[...]))
        return _
    lax.fori_loop(0, 4, chunk, 0)


def ffn_bwd_in(c, gb_ref, win, wout, dfac_ref, acc_ref, qht_ref, put, vec):
    for r in range(0, L, 256):
        rows = slice(r, r + 256)
        gp = (nt(gb_ref[rows, :], wout[...]) * dfac_ref[c, rows, :].astype(F32)).astype(BF)
        dfac_ref[c, rows, :] = gp
        vec[pl.ds(8 + c, 1), :] += jnp.sum(gp.astype(F32), axis=0, keepdims=True)
        acc_ref[rows, :] += nt(gp, win[...])
    put(nn(qht_ref[...], dfac_ref[c]))


def ln1_bwd(acc_ref, gs_ref, slh_ref, n1_ref, r1_ref, sm, gat_ref, vec):
    def f(r):
        rows = pl.ds(r, 64)
        gh = gs_ref[rows, :] + acc_ref[rows, :] * slh_ref[rows, :].astype(F32)
        n = n1_ref[rows, :]
        colsum(vec, 3, gh * n)
        colsum(vec, 5, gh)
        q = gh * sm[3:4, :]
        gs = r1_ref[rows, 0:1] * (q - mean(q) - n * mean(q * n))
        gs_ref[rows, :] = gs
        gat = gs.astype(BF)
        gat_ref[rows, :] = gat
        colsum(vec, 2, gat.astype(F32))
    rows_loop(L, 64, f)


def out_bwd(gat_ref, wo_ref, qct_ref, slc_ref, dc_ref, dct_ref, put):
    put(nn(qct_ref[...], gat_ref[...]))
    g = nt(gat_ref[...], wo_ref[...])
    for p in range(NP):
        cols = slice(p * 128, (p + 1) * 128)
        d = (g[:, cols] * slc_ref[:, cols].astype(F32)).astype(BF)
        dc_ref[p] = d
        dct_ref[p] = d.T


def attn_bwd(q_ref, k_t, v_ref, dc_ref, dc_t, p_ref, dq_ref, dk_ref, dv_ref, service):
    low = lax.broadcasted_iota(jnp.int32, (128, L), 0) < 64
    lane_low = lax.broadcasted_iota(jnp.int32, (L, 128), 1) < 64

    def pair(p, c):
        qp, kt, vp, dc, dct = q_ref[p], k_t[p], v_ref[p], dc_ref[p], dc_t[p]
        res = []
        for t in range(2):
            dm = jnp.where(low if t == 0 else ~low, dct, jnp.zeros_like(dct))
            dp = nn(vp, dm)
            pr = p_ref[2 * p + t]
            prf = pr.astype(F32)
            delta = jnp.sum(dp * prf, axis=0, keepdims=True)
            ds = (prf * (dp - delta)).astype(BF)
            res.append((nn(pr, dc), nn(ds, qp), nn(kt[64 * t:64 * t + 64, :], ds) * 0.125))
        dv_ref[p] = jnp.where(lane_low, res[0][0], res[1][0]).astype(BF)
        dk_ref[p] = jnp.where(lane_low, res[0][1], res[1][1]).astype(BF)
        dq_ref[p] = jnp.concatenate([res[0][2], res[1][2]], axis=0).astype(BF).T
        service(p)
        return c
    lax.fori_loop(0, NP, pair, 0)


def qkv_bwd(qi_ref, qit_ref, x_ref, w_ref, dq_ref, dk_ref, dv_ref, gs_ref, acc_ref, put, vec, b0, i0):
    for p in range(NP):
        qit_ref[p * 128:(p + 1) * 128, :] = qi_ref[:, p * 128:(p + 1) * 128].T
    for m, ref in enumerate((dq_ref, dk_ref, dv_ref)):
        d = jnp.concatenate([ref[p] for p in range(NP)], axis=1)
        put(m, nn(qit_ref[...], d))
        if m != 1:
            colsum(vec, 0 if m == 0 else 1, d.astype(F32))
        if m == 0:
            acc_ref[...] = nt(d, w_ref[m])
        else:
            acc_ref[...] += nt(d, w_ref[m])

    def f(r):
        rows = pl.ds(r, 64)
        th = jnp.tanh(x_ref[rows, :].astype(F32) * i0)
        x_ref[rows, :] = (gs_ref[rows, :] + acc_ref[rows, :] * (1.0 - th * th)).astype(BF)
    rows_loop(L, 64, f)


MESH = pl.DeviceIdType.MESH


def fused_kernel(n_dp, tok, cot, len_ref, rng_ref, wqkv, wo, win, wout, sm,
                 outp, gxp, gw, vout,
                 w, g, x_ref, ct_ref, qi_ref, q_ref, k_ref, v_ref, qt_ref, kt_ref, vt_ref, p_ref, ctxt_ref, qct_ref, slc_ref,
                 n1_ref, r1_ref, hid_ref, slh_ref, qh_ref, act_ref, dfac_ref, acc_ref, gb_ref, za, vec, vrecv, *rest):
    nb = n_dp.bit_length() - 1
    bufs, (wsem, locsem, a2s, a2r, gs_sem, gr_sem, zs_sem, zr_sem, vs_sem, vr_sem) = rest[:nb], rest[nb:]
    rs, nz, SEG = D // n_dp, 4, L // 4
    dp, z = lax.axis_index("dp"), lax.axis_index("head")
    bit = [(dp // (1 << b)) % 2 for b in range(nb)]
    buddy = [dp + (1 - 2 * bit[b]) * (1 << b) for b in range(nb)]
    z_near, z_cross, z_far = z + 1 - 2 * (z % 2), 3 - z, (z + 2) % 4
    peers = (z_near, z_far, z_cross)
    inner = (z + 1) // 2 == 1

    def at(dpi, zi):
        return {"dp": dpi, "head": zi}

    def load_w(slot, src):
        return pltpu.make_async_copy(src, w.at[slot], wsem.at[slot])

    def win_c(c):
        return win.at[:, pl.ds(pl.multiple_of(c * D, D), D)]

    def wout_c(c):
        return wout.at[pl.ds(pl.multiple_of(c * D, D), D), :]

    def seg(i):
        return pl.ds(pl.multiple_of(i * SEG, SEG), SEG)

    def to_seq(n, src, dst, j):
        return pltpu.make_async_remote_copy(src.at[peers[j]], dst.at[seg(z), :], a2s.at[n, j], a2r.at[n, j], device_id=at(dp, peers[j]),
                                            device_id_type=MESH)

    def to_seq_in(n, src, dst, j):
        return pltpu.make_async_remote_copy(src.at[peers[j]], dst.at[seg(peers[j]), :], a2s.at[n, j], a2r.at[n, j],
                                            device_id=at(dp, peers[j]), device_id_type=MESH)

    def to_pos(n, src, dst, j):
        return pltpu.make_async_remote_copy(src.at[seg(peers[j]), :], dst.at[z], a2s.at[n, j], a2r.at[n, j], device_id=at(dp, peers[j]),
                                            device_id_type=MESH)

    def to_pos_in(n, src, dst, j):
        return pltpu.make_async_remote_copy(src.at[seg(peers[j]), :], dst.at[peers[j]], a2s.at[n, j], a2r.at[n, j],
                                            device_id=at(dp, peers[j]), device_id_type=MESH)

    full = [g.reshape(*((8,) + (2,) * nb + (rs, D)))] + list(bufs)

    def order(i):
        up = list(range(1, nb))
        return [0] + (up if i % 2 == 0 else up[::-1])

    def slot(i, k):
        return i % 8 if k < 1 else i

    def pick(i, k, **vals):
        left = sorted(set(range(nb)) - set(order(i)[:k]), reverse=True)
        return (slot(i, k),) + tuple(vals.get(f"b{b}", slice(None)) for b in left)

    def red(i, k):
        b = order(i)[k]
        return pltpu.make_async_remote_copy(full[k].at[pick(i, k, **{f"b{b}": 1 - bit[b]})], full[k + 1].at[slot(i, k + 1)], gs_sem.at[k, i],
                                            gr_sem.at[k, i], device_id=at(buddy[b], z), device_id_type=MESH)

    def red_add(i, k):
        b = order(i)[k]
        red(i, k).wait_recv()
        if k + 1 < nb:
            n = order(i)[k + 1]
            for val in (1 - bit[n], bit[n]):
                d = pick(i, k + 1, **{f"b{n}": val})
                s = pick(i, k, **{f"b{b}": bit[b], f"b{n}": val})
                full[k + 1][d] = full[k + 1][d] + full[k][s]
                if val is not bit[n]:
                    red(i, k + 1).start()
        else:
            full[nb][i] = full[nb][i] + full[k][pick(i, k, **{f"b{b}": bit[b]})]
            pl.when(jnp.logical_not(inner))(zcopy(i, 0).start)

    def zcopy(i, k):
        src, dst, to = ((bufs[nb - 1], za, z_near), (za, gw, z_cross), (gw, gw, z_near))[k]
        return pltpu.make_async_remote_copy(src.at[i], dst.at[i], zs_sem.at[k, i], zr_sem.at[k, i], device_id=at(dp, to), device_id_type=MESH)

    def z_add(i, k):
        @pl.when(inner)
        def _():
            zcopy(i, k).wait_recv()
            if k == 0:
                za[i] = za[i] + bufs[nb - 1][i]
                zcopy(i, 1).start()
            else:
                gw[i] = gw[i] + za[i]
                zcopy(i, 2).start()

    def z_end(i):
        @pl.when(inner)
        def _():
            zcopy(i, 1).wait_send()
            zcopy(i, 2).wait_send()

        @pl.when(jnp.logical_not(inner))
        def _():
            zcopy(i, 2).wait_recv()
            zcopy(i, 0).wait_send()

    def vcopy(k):
        if k < nb:
            src, dst, to = vec.at[k], vrecv.at[k], at(buddy[k], z)
        else:
            src, dst, to = ((vec.at[nb], vrecv.at[nb], at(dp, z_near)), (vec.at[nb + 1], vrecv.at[nb + 1], at(dp, z_cross)),
                            (vout, vout, at(dp, z_near)))[k - nb]
        return pltpu.make_async_remote_copy(src, dst, vs_sem.at[k], vr_sem.at[k], device_id=to, device_id_type=MESH)

    def v_add(k):
        if k < nb:
            vcopy(k).wait_recv()
            vec[k + 1] = vec[k] + vrecv[k]
            if k + 1 < nb:
                vcopy(k + 1).start()
            else:
                pl.when(jnp.logical_not(inner))(vcopy(nb).start)
        else:
            @pl.when(inner)
            def _():
                vcopy(k).wait_recv()
                if k == nb:
                    vec[nb + 1] = vec[nb] + vrecv[nb]
                    vcopy(nb + 1).start()
                else:
                    vout[...] = vec[nb + 1] + vrecv[nb + 1]
                    vcopy(nb + 2).start()

    def v_end():
        for k in range(nb):
            vcopy(k).wait_send()

        @pl.when(inner)
        def _():
            vcopy(nb + 1).wait_send()
            vcopy(nb + 2).wait_send()

        @pl.when(jnp.logical_not(inner))
        def _():
            vcopy(nb).wait_send()
            vcopy(nb + 2).wait_recv()

    for m in range(3):
        load_w(m, wqkv.at[m]).start()
    own_tok = pltpu.make_async_copy(tok.at[z], x_ref.at[seg(z), :], locsem.at[0])
    own_tok.start()
    load_w(3, wo).start()
    load_w(4, win_c(0)).start()
    load_w(5, wout_c(0)).start()
    barrier = pltpu.get_barrier_semaphore()
    others = [at(buddy[b], z) for b in range(nb)] + [at(dp, p) for p in peers]
    for o in others:
        pl.semaphore_signal(barrier, inc=1, device_id=o, device_id_type=MESH)
    pl.semaphore_wait(barrier, len(others))
    for j in (1, 2, 0):
        to_seq(0, tok, x_ref, j).start()
    b = [jnp.full((1, 1), rng_ref[i], jnp.int32).astype(F32) * (1 / 16.0) for i in range(4)]
    iv = [1.0 / t for t in b]
    vec[0] = jnp.zeros_like(vec[0])
    v0 = vec.at[0]

    own_tok.wait()
    for m in range(3):
        load_w(m, wqkv.at[m]).wait()
    for j in range(4):
        if j:
            to_seq_in(0, tok, x_ref, j - 1).wait_recv()
        qkv(x_ref, qi_ref, w, sm, q_ref, k_ref, v_ref, qt_ref, kt_ref, vt_ref, b[0], iv[0], seg(peers[j - 1] if j else z))
    own_cot = pltpu.make_async_copy(cot.at[z], ct_ref.at[seg(z), :], locsem.at[1])
    own_cot.start()
    for j in (1, 2, 0):
        to_seq(1, cot, ct_ref, j).start()
    load_w(0, win_c(1)).start()
    load_w(1, wout_c(1)).start()
    attn_fwd(qt_ref, k_ref, vt_ref, p_ref, ctxt_ref, len_ref[z])
    load_w(3, wo).wait()
    out_proj(ctxt_ref, x_ref, w.at[3], sm, qct_ref, slc_ref, n1_ref, r1_ref, hid_ref, slh_ref, qh_ref, acc_ref, b[1], iv[1], b[2], iv[2])

    def w_slot(c):
        return 4 * (1 - c % 2)

    def fwd_wait(c):
        load_w(w_slot(c), win_c(c)).wait()
        load_w(w_slot(c) + 1, wout_c(c)).wait()
        return w_slot(c)

    def fwd_done(c):
        @pl.when(c < 2)
        def _():
            load_w(w_slot(c), win_c(c + 2)).start()
            load_w(w_slot(c) + 1, wout_c(c + 2)).start()

    ffn_fwd(qh_ref, w, sm, act_ref, dfac_ref, acc_ref, b[3], iv[3], fwd_wait, fwd_done)
    own_cot.wait()
    for j in range(3):
        to_seq_in(1, cot, ct_ref, j).wait_recv()
    ln2(acc_ref, hid_ref, ct_ref, sm, gb_ref, v0)
    own_out = pltpu.make_async_copy(ct_ref.at[seg(z), :], outp.at[z], locsem.at[2])
    own_out.start()
    for j in (1, 2, 0):
        to_pos(2, ct_ref, outp, j).start()

    def put_out(c, v):
        fr = 4 * rs
        for h in range(D // fr):
            for j in range(4):
                g[j, c * (D // fr) + h] = v[h * fr + j * rs:h * fr + (j + 1) * rs].astype(BF)

    def put(i, v):
        g[i % 8] = v.astype(BF).reshape(n_dp, rs, D)

    ffn_bwd_out(gb_ref, qh_ref, act_ref, vt_ref.reshape(D, L), put_out)
    for i in range(4):
        red(i, 0).start()
    acc_ref[...] = jnp.zeros_like(acc_ref)
    qht = vt_ref.reshape(D, L)
    for j in range(4):
        c = 3 - j
        s = w_slot(c)
        if j >= 2:
            fwd_wait(c)
        ffn_bwd_in(c, gb_ref, w.at[s], w.at[s + 1], dfac_ref, acc_ref, qht, functools.partial(put, 4 + j), v0)
        red(4 + j, 0).start()
        if j < 2:
            load_w(s, win_c(c - 2)).start()
            load_w(s + 1, wout_c(c - 2)).start()
        if j == 2:
            load_w(0, wqkv.at[0]).start()
            load_w(1, wqkv.at[1]).start()
        red_add(j, 0)
    ln1_bwd(acc_ref, hid_ref, slh_ref, n1_ref, r1_ref, sm, gb_ref, v0)
    red_add(4, 0)
    red_add(5, 0)
    dc = LaneSlots(act_ref)
    red(0, 0).wait_send()
    out_bwd(gb_ref, w.at[3], qct_ref, slc_ref, dc, vt_ref, functools.partial(put, 8))
    red(8, 0).start()
    red_add(6, 0)
    red_add(7, 0)
    steps = {1: [(0, 1), (1, 1)], 2: [(8, 0)], 3: [(0, 2), (1, 2)], 5: [(2, 1), (3, 1)]}

    def service(p):
        for at_p, todo in steps.items():
            @pl.when(p == at_p)
            def _():
                for i, k in todo:
                    red_add(i, k)

    attn_bwd(q_ref, kt_ref, v_ref, dc, vt_ref, p_ref, q_ref, k_ref, v_ref, service)
    for i in (1, 2, 3):
        red(i, 0).wait_send()
    for m in (0, 1):
        load_w(m, wqkv.at[m]).wait()

    def put_q(m, v):
        put(9 + m, v)
        red(9 + m, 0).start()
        if m == 0:
            red_add(2, 2)
            red_add(3, 2)
            z_add(0, 0)
            z_add(1, 0)
        if m == 1:
            red_add(9, 0)
            z_add(0, 1)
            z_add(1, 1)
        if m == 2:
            red_add(10, 0)

    qkv_bwd(qi_ref, qct_ref, x_ref, w, q_ref, k_ref, v_ref, hid_ref, acc_ref, put_q, v0, b[0], iv[0])
    vcopy(0).start()
    own_gx = pltpu.make_async_copy(x_ref.at[seg(z), :], gxp.at[z], locsem.at[3])
    own_gx.start()
    for j in (1, 2, 0):
        to_pos(3, x_ref, gxp, j).start()

    red_add(11, 0)
    v_add(0)
    for pr in range(2, 7):
        for i in (2 * pr, 2 * pr + 1):
            if i < 12:
                red_add(i, 1)
        if pr == 2:
            z_add(2, 0)
            z_add(3, 0)
        for i in (2 * pr, 2 * pr + 1):
            if i < 12:
                red_add(i, 2)
        if pr == 2:
            z_add(2, 1)
            z_add(3, 1)
        if pr > 2:
            for i in (2 * pr - 2, 2 * pr - 1):
                z_add(i, 0)
            for i in (2 * pr - 4, 2 * pr - 3):
                if i >= 4:
                    z_add(i, 1)
        if pr - 1 < nb + 2:
            v_add(pr - 1)
    z_add(10, 1)
    z_add(11, 1)
    for i in range(12):
        z_end(i)
        for k in range(nb):
            if (k, i) not in ((0, 0), (0, 1), (0, 2), (0, 3)):
                red(i, k).wait_send()
    v_end()
    own_out.wait()
    own_gx.wait()
    for j in range(3):
        to_seq(0, tok, x_ref, j).wait_send()
        to_seq(1, cot, ct_ref, j).wait_send()
        to_pos(2, ct_ref, outp, j).wait_send()
        to_pos_in(2, ct_ref, outp, j).wait_recv()
        to_pos(3, x_ref, gxp, j).wait_send()
        to_pos_in(3, x_ref, gxp, j).wait_recv()


def fused(n_dp, *args):
    nb, rs = n_dp.bit_length() - 1, D // n_dp

    def vm(*s, d=BF):
        return pltpu.VMEM(s, d)
    dma = pltpu.SemaphoreType.DMA
    scratch = [vm(6, D, D), vm(8, n_dp, rs, D), vm(L, D), vm(L, D), vm(L, D), vm(6, L, 128), vm(6, L, 128), vm(6, L, 128), vm(6, 128, L),
               vm(6, 128, L), vm(6, 128, L), vm(12, L, L), vm(6, 128, L), vm(D, L), vm(L, D),
               vm(L, D, d=F32), vm(L, 128, d=F32), vm(L, D, d=F32), vm(L, D), vm(L, D), vm(4, L, D), vm(4, L, D), vm(L, D, d=F32),
               vm(L, D), vm(12, rs, D), vm(nb + 2, 16, D, d=F32), vm(nb + 2, 16, D, d=F32)]
    scratch += [vm(*((12,) + (2,) * (nb - k) + (rs, D))) for k in range(1, nb + 1)]
    scratch += [dma((6,)), dma((4,)), dma((4, 3)), dma((4, 3)), dma((nb, 12)), dma((nb, 12)), dma((3, 12)), dma((3, 12)), dma((nb + 3,)), dma((nb + 3,))]
    pos = jax.ShapeDtypeStruct((4, L // 4, D), BF)
    outs = [pos, pos, jax.ShapeDtypeStruct((12, rs, D), BF), jax.ShapeDtypeStruct((16, D), F32)]
    v, s, h = (pl.BlockSpec(memory_space=m) for m in (pltpu.VMEM, pltpu.SMEM, pl.ANY))
    return pl.pallas_call(
        functools.partial(fused_kernel, n_dp), out_shape=outs, in_specs=[h, h, s, s, h, h, h, h, v], out_specs=[h, h, v, v],
        scratch_shapes=scratch,
        compiler_params=pltpu.CompilerParams(collective_id=0, has_side_effects=True, vmem_limit_bytes=64 * 1024 * 1024 - 65536))(*args)


def on_device(n_dp, tokens, lengths, ranges, qkv_weight, qv_bias, out_weight, out_bias, norm_gains, norm_shifts, ffn_in, ffn_in_bias,
              ffn_out, ffn_out_bias, cotangent):
    small = jnp.concatenate([qv_bias, out_bias[None], norm_gains, norm_shifts, ffn_out_bias[None], ffn_in_bias.reshape(4, D)]).astype(F32)
    out, gx, gw, vec = fused(n_dp, tokens.transpose(1, 0, 2), cotangent.transpose(1, 0, 2), lengths, ranges, qkv_weight, out_weight,
                             ffn_in, ffn_out, small)
    rs = D // n_dp
    i = lax.axis_index("dp")
    gw = gw.astype(F32)

    def mine(v):
        return lax.dynamic_slice_in_dim(v, i * rs, rs, axis=-1)
    fib = lax.dynamic_slice(vec[8:12].reshape(-1), (i * 4 * rs,), (4 * rs,))
    return (out.transpose(1, 0, 2), gx.transpose(1, 0, 2).astype(F32), gw[9:12], mine(vec[0:2]), gw[8], mine(vec[2]), mine(vec[3:5]),
            mine(vec[5:7]), gw[7:3:-1].transpose(1, 0, 2).reshape(rs, F), fib, gw[0:4].reshape(4 * rs, D), mine(vec[7]))


def local_kernel(x_ref, ct_ref, len_ref, rng_ref, w_ref, sm, gx_ref, g_ref, vec_ref, w, qi_ref, q_ref, k_ref, v_ref, qt_ref, kt_ref, vt_ref,
                 p_ref, ctxt_ref, qct_ref, slc_ref, n1_ref, r1_ref, hid_ref, slh_ref, qh_ref, act_ref, dfac_ref, acc_ref, gb_ref, stage,
                 wsem, gsem):
    def fetch(slot, i):
        cp = pltpu.make_async_copy(w_ref.at[i], w.at[slot], wsem)
        cp.start()
        cp.wait()

    def put(i, v):
        stage[...] = v.astype(BF)
        cp = pltpu.make_async_copy(stage, g_ref.at[i], gsem)
        cp.start()
        cp.wait()

    b = [jnp.full((1, 1), rng_ref[i], jnp.int32).astype(F32) * (1 / 16.0) for i in range(4)]
    iv = [1.0 / t for t in b]
    vec_ref[...] = jnp.zeros_like(vec_ref)
    for m in range(4):
        fetch(m, 8 + (m + 1) % 4 if m < 3 else 8)
    for r in range(0, L, 256):
        qkv(x_ref, qi_ref, w, sm, q_ref, k_ref, v_ref, qt_ref, kt_ref, vt_ref, b[0], iv[0], slice(r, r + 256))
    attn_fwd(qt_ref, k_ref, vt_ref, p_ref, ctxt_ref, len_ref[0])
    out_proj(ctxt_ref, x_ref, w.at[3], sm, qct_ref, slc_ref, n1_ref, r1_ref, hid_ref, slh_ref, qh_ref, acc_ref, b[1], iv[1], b[2], iv[2])

    def before(c):
        fetch(4, c)
        fetch(5, 4 + c)
        return 4

    ffn_fwd(qh_ref, w, sm, act_ref, dfac_ref, acc_ref, b[3], iv[3], before, lambda c: None)
    ln2(acc_ref, hid_ref, ct_ref, sm, gb_ref, vec_ref)
    qht = vt_ref.reshape(D, L)
    ffn_bwd_out(gb_ref, qh_ref, act_ref, qht, lambda c, v: put(4 + c, v))
    acc_ref[...] = jnp.zeros_like(acc_ref)
    for c in range(4):
        before(c)
        ffn_bwd_in(c, gb_ref, w.at[4], w.at[5], dfac_ref, acc_ref, qht, functools.partial(put, c), vec_ref)
    ln1_bwd(acc_ref, hid_ref, slh_ref, n1_ref, r1_ref, sm, gb_ref, vec_ref)
    dc = LaneSlots(act_ref)
    out_bwd(gb_ref, w.at[3], qct_ref, slc_ref, dc, vt_ref, functools.partial(put, 8))
    attn_bwd(q_ref, kt_ref, v_ref, dc, vt_ref, p_ref, q_ref, k_ref, v_ref, lambda p: None)
    qkv_bwd(qi_ref, qct_ref, x_ref, w, q_ref, k_ref, v_ref, hid_ref, acc_ref, lambda m, v: put(9 + m, v), vec_ref, b[0], iv[0])
    gx_ref[...] = x_ref[...]


def local(x, ct, length, ranges, weights, small):
    def vm(*s, d=BF):
        return pltpu.VMEM(s, d)
    scratch = [vm(6, D, D), vm(L, D), vm(6, L, 128), vm(6, L, 128), vm(6, L, 128), vm(6, 128, L),
               vm(6, 128, L), vm(6, 128, L), vm(12, L, L), vm(6, 128, L), vm(D, L), vm(L, D),
               vm(L, D, d=F32), vm(L, 128, d=F32), vm(L, D, d=F32), vm(L, D), vm(L, D), vm(4, L, D), vm(4, L, D), vm(L, D, d=F32),
               vm(L, D), vm(D, D), pltpu.SemaphoreType.DMA, pltpu.SemaphoreType.DMA]
    outs = [jax.ShapeDtypeStruct((L, D), BF), jax.ShapeDtypeStruct((L, D), BF), jax.ShapeDtypeStruct((12, D, D), BF),
            jax.ShapeDtypeStruct((16, D), F32)]
    v, s, h = (pl.BlockSpec(memory_space=m) for m in (pltpu.VMEM, pltpu.SMEM, pl.ANY))

    def body(x_in, ct_in, len_ref, rng_ref, w_ref, sm, out_ref, gx_ref, g_ref, vec_ref, x_ref, *rest):
        x_ref[...] = x_in[...]
        out_ref[...] = ct_in[...]
        local_kernel(x_ref, out_ref, len_ref, rng_ref, w_ref, sm, gx_ref, g_ref, vec_ref, *rest)

    return pl.pallas_call(
        body, out_shape=outs, in_specs=[v, v, s, s, h, v], out_specs=[v, v, h, v], scratch_shapes=[vm(L, D)] + scratch,
        compiler_params=pltpu.CompilerParams(vmem_limit_bytes=60 * 1024 * 1024))(x, ct, length, ranges, weights, small)


def on_device_local(n_dp, tokens, lengths, ranges, qkv_weight, qv_bias, out_weight, out_bias, norm_gains, norm_shifts, ffn_in, ffn_in_bias,
                    ffn_out, ffn_out_bias, cotangent):
    def to_seq(a):
        return lax.all_to_all(a.transpose(1, 0, 2), "head", split_axis=0, concat_axis=1, tiled=True)[0]

    def to_pos(a):
        return lax.all_to_all(a[None], "head", split_axis=1, concat_axis=0, tiled=True).transpose(1, 0, 2)

    small = jnp.concatenate([qv_bias, out_bias[None], norm_gains, norm_shifts, ffn_out_bias[None], ffn_in_bias.reshape(4, D)]).astype(F32)
    weights = jnp.concatenate([ffn_in.reshape(D, 4, D).transpose(1, 0, 2), ffn_out.reshape(4, D, D), out_weight[None], qkv_weight])
    length = lax.dynamic_slice(lengths, (lax.axis_index("head"),), (1,))
    out, gx, g, vec = local(to_seq(tokens), to_seq(cotangent), length, ranges, weights, small)
    rs = D // n_dp
    wout = lax.psum_scatter(g[4:8].reshape(4 * D, D), "dp", scatter_dimension=0, tiled=True)
    rest = lax.psum_scatter(jnp.concatenate([g[0:4], g[8:12]]), "dp", scatter_dimension=1, tiled=True)
    both = lax.psum(jnp.concatenate([wout, rest.reshape(8 * rs, D)]), "head").astype(F32)
    wout, rest = both[:4 * rs], both[4 * rs:].reshape(8, rs, D)
    vec = lax.psum(vec, ("dp", "head"))
    i = lax.axis_index("dp")

    def mine(v):
        return lax.dynamic_slice_in_dim(v, i * rs, rs, axis=-1)
    fib = lax.dynamic_slice(vec[8:12].reshape(-1), (i * 4 * rs,), (4 * rs,))
    return (to_pos(out), to_pos(gx).astype(F32), rest[5:8], mine(vec[0:2]), rest[4], mine(vec[2]), mine(vec[3:5]), mine(vec[5:7]),
            rest[0:4].transpose(1, 0, 2).reshape(rs, F), fib, wout, mine(vec[7]))


def solution(mesh):
    n_dp = mesh.shape["dp"]
    tok = P("head", "dp", None)
    body = on_device if D // n_dp % 16 == 0 else on_device_local
    return jax.shard_map(
        functools.partial(body, n_dp),
        mesh=mesh,
        in_specs=(tok, P("dp")) + (P(),) * 11 + (tok,),
        out_specs=(tok, tok, P(None, "dp", None), P(None, "dp"), P("dp", None), P("dp"), P(None, "dp"), P(None, "dp"),
                   P("dp", None), P("dp"), P("dp", None), P("dp")),
        check_vma=False,
    )
```

time: 378 us -> 193 us (0.51)
  waiting for transfers between devices: 146 us -> 0 us
  Pallas kernels: 65.6 us -> 175 us
  blocking collectives: 59.9 us -> 0 us
  local copies, waits for them, and re-layouts: 49.2 us -> 15.5 us
  other arithmetic: 23.6 us -> 1.08 us
  starting transfers between devices: 19.1 us -> 0 us
  between operations: 13.9 us -> 0.82 us
    reduce_scatter x2 -> x0, waiting for transfers between devices: 111 us -> none  [the longest x1 80.4 us: on_device(): lax.psum_scatter(jnp.concatenate([g[0:4], g[8:12]]), 'dp', scatter_dimens...]
    pallas_call x1, Pallas kernels: 65.6 us -> 175 us  [fused(): pl.pallas_call(functools.partial(fused_kernel, n_dp), out_shape=outs, in_...]
    psum x1 -> x0, blocking collectives: 59.9 us -> none  [on_device(): vec = lax.psum(vec, ('dp', 'head'))]
    all_to_all x4 -> x0, waiting for transfers between devices: 22.4 us -> none  [the longest x2 22.4 us: to_seq(): lax.all_to_all(a.transpose(1, 0, 2), 'head', split_axis=0, concat_axis=1,...]
    all_to_all x4 -> x0, starting transfers between devices: 18.8 us -> none  [the longest x2 10.5 us: to_seq(): lax.all_to_all(a.transpose(1, 0, 2), 'head', split_axis=0, concat_axis=1,...]
    slice x4 -> x2, local copies, waits for them, and re-layouts: 15.2 us -> 2.14 us  [the longest x1 1.17 us: on_device(): gw[0:4].reshape(4 * rs, D)]
    concatenate x3 -> x0, other arithmetic: 12.8 us -> none  [the longest x1 9.38 us: on_device(): jnp.concatenate([g[0:4], g[8:12]])]
    psum x1 -> x0, waiting for transfers between devices: 12.7 us -> none  [on_device(): lax.psum(jnp.concatenate([wout, rest.reshape(8 * rs, D)]), 'head')]
  transfers between devices with their start and end apart: 7 -> 0, of which waited for: 5 -> 0; matrix products, arithmetic and copies ran while one was open for 14% -> 0% of each run, Pallas kernels for 0% -> 0%
where the time goes in v2:
time: 193 us; the launch traced here: 192 us
  Pallas kernels  175 us (91%)
  local copies, waits for them, and re-layouts  15.5 us (8%)
    pallas_call x1, Pallas kernels, fused(): pl.pallas_call(functools.partial(fused_kernel, n_dp), out_shape=outs, in_...  175 us
    unnamed x21, local copies, waits for them, and re-layouts  4.97 us

profile of v2, /device:TPU:0, one launch (start us, length us, event | category | flops | bytes accessed | tf_op | source)
XLA Modules:
  0.0 192.4 jit_solution(2085355493519632777)
XLA Ops:
  0.6 0.0 copy-start.4
  0.7 0.0 copy-start.7
  0.7 0.0 copy-start.5
  0.7 0.0 copy-start.6
  0.7 0.0 copy-start.8
  0.7 0.0 copy-start.3
  0.7 2.7 %copy_bitcast_fusion = (bf16[4,128,768]{2,1,0:T(8,128)(2,1)}, bf16[4,128,768]{2,1,0:T(8,128)(2,1)}) fusion(bf16[128,4,768]{2,1,0:T(4,128)(2,1)} %param.27, bf16[128,4,768]{2,1,0:T(4,128)(2,1)} %param.14), kind=kLoop, calls=%fused_computation.2 | loop fusion | bytes 3145728 | tf_op jit(solution)/shard_map/transpose | solution.py:588
  3.5 0.0 copy-done.7
  3.5 0.0 copy-done.8
  3.5 0.0 copy-done.3
  3.5 0.0 copy-done.4
  3.5 0.0 copy-done.5
  3.5 0.0 copy-done.6
  3.5 0.1 concatenate.3
  3.6 0.6 convert_element_type.12.sm
  4.2 174.9 %shard_map.229 = (bf16[4,128,768]{2,1,0:T(8,128)(2,1)}, bf16[4,128,768]{2,1,0:T(8,128)(2,1)}, bf16[12,96,768]{2,1,0:T(8,128)(2,1)}, f32[16,768]{1,0:T(8,128)}) custom-call(bf16[4,128,768]{2,1,0:T(8,128)(2,1)} %get-tuple-element.52.tok, bf16[4,128,768]{2,1,0:T(8,128)(2,1)} %get-tuple-element.51.cot, s32[4]{0:T(128)} %len_ref.1, s32[4]{0:T(128)} %rng_ref.1, ...), custom_call_target="tpu_custom_call" | custom-call | tf_op jit(solution)/shard_map/pallas_call | solution.py:579
  179.1 0.0 copy-start.1
  179.2 2.7 %copy.33 = bf16[128,4,768]{2,1,0:T(4,128)(2,1)} copy(bf16[128,4,768]{2,0,1:T(8,128)(2,1)} %bitcast.20) | data formatting | bytes 1572864
  181.9 0.0 copy-done.1
  181.9 0.1 convert_bitcast_fusion
  182.0 0.0 copy-start
  182.0 2.2 %copy.34 = f32[128,4,768]{2,1,0:T(4,128)} copy(f32[128,4,768]{2,0,1:T(8,128)S(1)} %convert_bitcast_fusion) | data formatting | bytes 3145728
  184.2 0.0 copy-start.2
  184.2 0.0 copy-done
  184.2 1.0 slice.40
  185.1 0.0 copy-done.2
  185.2 0.6 constant_dynamic-slice_fusion.4
  185.8 0.3 convert_element_type.15
  186.1 0.7 slice_bitcast_fusion
  186.9 0.6 fusion
  187.5 0.6 constant_dynamic-slice_fusion.2
  188.1 0.6 constant_dynamic-slice_fusion.1
  188.7 1.2 fusion.2
  189.9 0.1 reverse_bitcast_fusion
  190.0 1.1 copy.35
  191.1 0.7 dynamic_slice.27
  191.8 0.6 fusion.1
  (7 shorter events, 0.1 us)
Async XLA Ops:
  0.6 2.9 %copy-start.4 = (bf16[2,768]{1,0:T(2,128)(2,1)S(1)}, bf16[2,768]{1,0:T(2,128)(2,1)}, u32[]{:S(2)}) copy-start(bf16[2,768]{1,0:T(2,128)(2,1)} %param.18) | copy-start | bytes 9220
  0.7 2.8 %copy-start.7 = (bf16[768]{0:T(1024)(128)(2,1)S(1)}, bf16[768]{0:T(1024)(128)(2,1)}, u32[]{:S(2)}) copy-start(bf16[768]{0:T(1024)(128)(2,1)} %param.20) | copy-start | bytes 4612
  0.7 2.9 %copy-start.5 = (bf16[2,768]{1,0:T(2,128)(2,1)S(1)}, bf16[2,768]{1,0:T(2,128)(2,1)}, u32[]{:S(2)}) copy-start(bf16[2,768]{1,0:T(2,128)(2,1)} %param.21) | copy-start | bytes 9220
  0.7 2.9 %copy-start.6 = (bf16[2,768]{1,0:T(2,128)(2,1)S(1)}, bf16[2,768]{1,0:T(2,128)(2,1)}, u32[]{:S(2)}) copy-start(bf16[2,768]{1,0:T(2,128)(2,1)} %param.22) | copy-start | bytes 9220
  0.7 2.8 %copy-start.8 = (bf16[768]{0:T(1024)(128)(2,1)S(1)}, bf16[768]{0:T(1024)(128)(2,1)}, u32[]{:S(2)}) copy-start(bf16[768]{0:T(1024)(128)(2,1)} %param.26) | copy-start | bytes 4612
  0.7 2.8 %copy-start.3 = (bf16[3072]{0:T(1024)(128)(2,1)S(1)}, bf16[3072]{0:T(1024)(128)(2,1)}, u32[]{:S(2)}) copy-start(bf16[3072]{0:T(1024)(128)(2,1)} %param.24) | copy-start | bytes 18436
  179.1 2.7 %copy-start.1 = (bf16[4,128,768]{2,1,0:T(8,128)(2,1)S(1)}, bf16[4,128,768]{2,1,0:T(8,128)(2,1)}, u32[]{:S(2)}) copy-start(bf16[4,128,768]{2,1,0:T(8,128)(2,1)} %get-tuple-element.17) | copy-start | bytes 2359300
  182.0 2.2 %copy-start = (bf16[12,96,768]{2,1,0:T(8,128)(2,1)S(1)}, bf16[12,96,768]{2,1,0:T(8,128)(2,1)}, u32[]{:S(2)}) copy-start(bf16[12,96,768]{2,1,0:T(8,128)(2,1)} %get-tuple-element.18) | copy-start | bytes 5308420
  184.2 1.0 copy-start.2

commit v3 on v2

--- a/solution.py
+++ b/solution.py
@@ -45,10 +45,11 @@
         self.ref[0, :, pl.ds(pl.multiple_of(p * 128, 128), 128)] = value
 
 
-def qkv(x_ref, qi_ref, w_ref, sm, q_ref, k_ref, v_ref, qt_ref, kt_ref, vt_ref, b0, r0, rows):
+def qkv(x_ref, qit_ref, w_ref, sm, q_ref, k_ref, v_ref, qt_ref, kt_ref, vt_ref, b0, r0, rows):
     xb = x_ref[rows, :].astype(F32)
     qi = (b0 * jnp.tanh(xb * r0)).astype(BF)
-    qi_ref[rows, :] = qi
+    for p in range(NP):
+        qit_ref[p * 128:(p + 1) * 128, rows] = qi[:, p * 128:(p + 1) * 128].T
     for m, (dst, tdst) in enumerate(((q_ref, qt_ref), (k_ref, kt_ref), (v_ref, vt_ref))):
         y = nn(qi, w_ref[m])
         if m == 0:
@@ -148,10 +149,7 @@
     rows_loop(L, 64, f)
 
 
-def ffn_bwd_out(gb_ref, qh_ref, act_ref, qht_ref, put):
-    for p in range(NP):
-        qht_ref[p * 128:(p + 1) * 128, :] = qh_ref[:, p * 128:(p + 1) * 128].T
-
+def ffn_bwd_out(gb_ref, act_ref, put):
     def chunk(c, _):
         put(c, tn(act_ref[c], gb_ref[...]))
         return _
@@ -217,14 +215,15 @@
     lax.fori_loop(0, NP, pair, 0)
 
 
-def qkv_bwd(qi_ref, qit_ref, x_ref, w_ref, dq_ref, dk_ref, dv_ref, gs_ref, acc_ref, put, vec, b0, i0):
-    for p in range(NP):
-        qit_ref[p * 128:(p + 1) * 128, :] = qi_ref[:, p * 128:(p + 1) * 128].T
+def lanes(ref):
+    return jnp.concatenate([ref[p] for p in range(NP)], axis=1)
+
+
+def qkv_bwd_x(x_ref, w_ref, dq_ref, dk_ref, dv_ref, gs_ref, acc_ref, vec, i0):
     for m, ref in enumerate((dq_ref, dk_ref, dv_ref)):
-        d = jnp.concatenate([ref[p] for p in range(NP)], axis=1)
-        put(m, nn(qit_ref[...], d))
+        d = lanes(ref)
         if m != 1:
-            colsum(vec, 0 if m == 0 else 1, d.astype(F32))
+            colsum(vec, m // 2, d.astype(F32))
         if m == 0:
             acc_ref[...] = nt(d, w_ref[m])
         else:
@@ -238,11 +237,29 @@
 
 
 MESH = pl.DeviceIdType.MESH
+SCHEDULE = {
+    "f0": [(0, 0)],
+    "f1": [(0, 1)],
+    "f2": [(0, 4)],
+    "ln": [(1, 0), (0, 5)],
+    "a0": [(1, 1)],
+    "a1": [(2, 0), (0, 7), (0, 3), (0, 6)],
+    "a3": [(2, 1)],
+    "a5": [(3, 0), (1, 5)],
+    "x": [(9, 1), (0, 2), (4, 0)],
+    "q0": [(9, 2), (1, 4), (2, 5), (0, 9), (1, 7)],
+    "q1": [(0, 8), (3, 5), (1, 2), (9, 0), (3, 1), (1, 3)],
+    "q2": [(2, 7), (4, 5), (0, 11), (1, 9)],
+    "drain": [(3, 7), (2, 4), (4, 1), (2, 2), (0, 10), (2, 3), (3, 4), (2, 9), (4, 7), (3, 2), (1, 6), (4, 4), (3, 3), (1, 8),
+        (1, 11), (4, 2), (1, 10), (3, 9), (2, 6), (4, 3), (2, 11), (3, 6), (4, 9), (3, 11), (2, 10), (2, 8), (4, 6), (3, 10), (4, 11),
+        (3, 8), (4, 10), (4, 8)],
+}
+V_WITH = 9
 
 
 def fused_kernel(n_dp, tok, cot, len_ref, rng_ref, wqkv, wo, win, wout, sm,
                  outp, gxp, gw, vout,
-                 w, g, x_ref, ct_ref, qi_ref, q_ref, k_ref, v_ref, qt_ref, kt_ref, vt_ref, p_ref, ctxt_ref, qct_ref, slc_ref,
+                 w, g, x_ref, ct_ref, qit_ref, q_ref, k_ref, v_ref, qt_ref, kt_ref, vt_ref, p_ref, ctxt_ref, qct_ref, slc_ref,
                  n1_ref, r1_ref, hid_ref, slh_ref, qh_ref, act_ref, dfac_ref, acc_ref, gb_ref, za, vec, vrecv, *rest):
     nb = n_dp.bit_length() - 1
     bufs, (wsem, locsem, a2s, a2r, gs_sem, gr_sem, zs_sem, zr_sem, vs_sem, vr_sem) = rest[:nb], rest[nb:]
@@ -346,7 +363,7 @@
 
     def vcopy(k):
         if k < nb:
-            src, dst, to = vec.at[k], vrecv.at[k], at(buddy[k], z)
+            src, dst, to = vec.at[k], vrecv.at[k], at(buddy[order(V_WITH)[k]], z)
         else:
             src, dst, to = ((vec.at[nb], vrecv.at[nb], at(dp, z_near)), (vec.at[nb + 1], vrecv.at[nb + 1], at(dp, z_cross)),
                             (vout, vout, at(dp, z_near)))[k - nb]
@@ -410,7 +427,7 @@
     for j in range(4):
         if j:
             to_seq_in(0, tok, x_ref, j - 1).wait_recv()
-        qkv(x_ref, qi_ref, w, sm, q_ref, k_ref, v_ref, qt_ref, kt_ref, vt_ref, b[0], iv[0], seg(peers[j - 1] if j else z))
+        qkv(x_ref, qit_ref, w, sm, q_ref, k_ref, v_ref, qt_ref, kt_ref, vt_ref, b[0], iv[0], seg(peers[j - 1] if j else z))
     own_cot = pltpu.make_async_copy(cot.at[z], ct_ref.at[seg(z), :], locsem.at[1])
     own_cot.start()
     for j in (1, 2, 0):
@@ -454,11 +471,25 @@
     def put(i, v):
         g[i % 8] = v.astype(BF).reshape(n_dp, rs, D)
 
-    ffn_bwd_out(gb_ref, qh_ref, act_ref, vt_ref.reshape(D, L), put_out)
+    def at_point(point):
+        for k, i in SCHEDULE.get(point, ()):
+            if k == 9:
+                to_pos(3, x_ref, gxp, i).start()
+            elif k < nb:
+                red_add(i, k)
+            else:
+                z_add(i, k - nb)
+            if i == V_WITH and k != 9:
+                v_add(k)
+
+    ffn_bwd_out(gb_ref, act_ref, put_out)
     for i in range(4):
         red(i, 0).start()
     acc_ref[...] = jnp.zeros_like(acc_ref)
     qht = vt_ref.reshape(D, L)
+    for p in range(NP):
+        qht[p * 128:(p + 1) * 128, :] = qh_ref[:, p * 128:(p + 1) * 128].T
+    at_point("fo")
     for j in range(4):
         c = 3 - j
         s = w_slot(c)
@@ -472,78 +503,36 @@
         if j == 2:
             load_w(0, wqkv.at[0]).start()
             load_w(1, wqkv.at[1]).start()
-        red_add(j, 0)
+        at_point(f"f{j}")
     ln1_bwd(acc_ref, hid_ref, slh_ref, n1_ref, r1_ref, sm, gb_ref, v0)
-    red_add(4, 0)
-    red_add(5, 0)
+    at_point("ln")
     dc = LaneSlots(act_ref)
     red(0, 0).wait_send()
     out_bwd(gb_ref, w.at[3], qct_ref, slc_ref, dc, vt_ref, functools.partial(put, 8))
     red(8, 0).start()
-    red_add(6, 0)
-    red_add(7, 0)
-    steps = {1: [(0, 1), (1, 1)], 2: [(8, 0)], 3: [(0, 2), (1, 2)], 5: [(2, 1), (3, 1)]}
+    at_point("ob")
 
     def service(p):
-        for at_p, todo in steps.items():
-            @pl.when(p == at_p)
-            def _():
-                for i, k in todo:
-                    red_add(i, k)
+        for at_p in range(NP):
+            if f"a{at_p}" in SCHEDULE:
+                @pl.when(p == at_p)
+                def _():
+                    at_point(f"a{at_p}")
 
     attn_bwd(q_ref, kt_ref, v_ref, dc, vt_ref, p_ref, q_ref, k_ref, v_ref, service)
-    for i in (1, 2, 3):
-        red(i, 0).wait_send()
     for m in (0, 1):
         load_w(m, wqkv.at[m]).wait()
-
-    def put_q(m, v):
-        put(9 + m, v)
-        red(9 + m, 0).start()
-        if m == 0:
-            red_add(2, 2)
-            red_add(3, 2)
-            z_add(0, 0)
-            z_add(1, 0)
-        if m == 1:
-            red_add(9, 0)
-            z_add(0, 1)
-            z_add(1, 1)
-        if m == 2:
-            red_add(10, 0)
-
-    qkv_bwd(qi_ref, qct_ref, x_ref, w, q_ref, k_ref, v_ref, hid_ref, acc_ref, put_q, v0, b[0], iv[0])
+    qkv_bwd_x(x_ref, w, q_ref, k_ref, v_ref, hid_ref, acc_ref, v0, iv[0])
     vcopy(0).start()
     own_gx = pltpu.make_async_copy(x_ref.at[seg(z), :], gxp.at[z], locsem.at[3])
     own_gx.start()
-    for j in (1, 2, 0):
-        to_pos(3, x_ref, gxp, j).start()
-
-    red_add(11, 0)
-    v_add(0)
-    for pr in range(2, 7):
-        for i in (2 * pr, 2 * pr + 1):
-            if i < 12:
-                red_add(i, 1)
-        if pr == 2:
-            z_add(2, 0)
-            z_add(3, 0)
-        for i in (2 * pr, 2 * pr + 1):
-            if i < 12:
-                red_add(i, 2)
-        if pr == 2:
-            z_add(2, 1)
-            z_add(3, 1)
-        if pr > 2:
-            for i in (2 * pr - 2, 2 * pr - 1):
-                z_add(i, 0)
-            for i in (2 * pr - 4, 2 * pr - 3):
-                if i >= 4:
-                    z_add(i, 1)
-        if pr - 1 < nb + 2:
-            v_add(pr - 1)
-    z_add(10, 1)
-    z_add(11, 1)
+    at_point("x")
+    for m, ref in enumerate((q_ref, k_ref, v_ref)):
+        red(1 + m, 0).wait_send()
+        put(9 + m, nn(qit_ref[...], lanes(ref)))
+        red(9 + m, 0).start()
+        at_point(f"q{m}")
+    at_point("drain")
     for i in range(12):
         z_end(i)
         for k in range(nb):
@@ -567,7 +556,7 @@
     def vm(*s, d=BF):
         return pltpu.VMEM(s, d)
     dma = pltpu.SemaphoreType.DMA
-    scratch = [vm(6, D, D), vm(8, n_dp, rs, D), vm(L, D), vm(L, D), vm(L, D), vm(6, L, 128), vm(6, L, 128), vm(6, L, 128), vm(6, 128, L),
+    scratch = [vm(6, D, D), vm(8, n_dp, rs, D), vm(L, D), vm(L, D), vm(D, L), vm(6, L, 128), vm(6, L, 128), vm(6, L, 128), vm(6, 128, L),
                vm(6, 128, L), vm(6, 128, L), vm(12, L, L), vm(6, 128, L), vm(D, L), vm(L, D),
                vm(L, D, d=F32), vm(L, 128, d=F32), vm(L, D, d=F32), vm(L, D), vm(L, D), vm(4, L, D), vm(4, L, D), vm(L, D, d=F32),
                vm(L, D), vm(12, rs, D), vm(nb + 2, 16, D, d=F32), vm(nb + 2, 16, D, d=F32)]
@@ -598,7 +587,7 @@
             mine(vec[5:7]), gw[7:3:-1].transpose(1, 0, 2).reshape(rs, F), fib, gw[0:4].reshape(4 * rs, D), mine(vec[7]))
 
 
-def local_kernel(x_ref, ct_ref, len_ref, rng_ref, w_ref, sm, gx_ref, g_ref, vec_ref, w, qi_ref, q_ref, k_ref, v_ref, qt_ref, kt_ref, vt_ref,
+def local_kernel(x_ref, ct_ref, len_ref, rng_ref, w_ref, sm, gx_ref, g_ref, vec_ref, w, qit_ref, q_ref, k_ref, v_ref, qt_ref, kt_ref, vt_ref,
                  p_ref, ctxt_ref, qct_ref, slc_ref, n1_ref, r1_ref, hid_ref, slh_ref, qh_ref, act_ref, dfac_ref, acc_ref, gb_ref, stage,
                  wsem, gsem):
     def fetch(slot, i):
@@ -618,7 +607,7 @@
     for m in range(4):
         fetch(m, 8 + (m + 1) % 4 if m < 3 else 8)
     for r in range(0, L, 256):
-        qkv(x_ref, qi_ref, w, sm, q_ref, k_ref, v_ref, qt_ref, kt_ref, vt_ref, b[0], iv[0], slice(r, r + 256))
+        qkv(x_ref, qit_ref, w, sm, q_ref, k_ref, v_ref, qt_ref, kt_ref, vt_ref, b[0], iv[0], slice(r, r + 256))
     attn_fwd(qt_ref, k_ref, vt_ref, p_ref, ctxt_ref, len_ref[0])
     out_proj(ctxt_ref, x_ref, w.at[3], sm, qct_ref, slc_ref, n1_ref, r1_ref, hid_ref, slh_ref, qh_ref, acc_ref, b[1], iv[1], b[2], iv[2])
 
@@ -630,7 +619,9 @@
     ffn_fwd(qh_ref, w, sm, act_ref, dfac_ref, acc_ref, b[3], iv[3], before, lambda c: None)
     ln2(acc_ref, hid_ref, ct_ref, sm, gb_ref, vec_ref)
     qht = vt_ref.reshape(D, L)
-    ffn_bwd_out(gb_ref, qh_ref, act_ref, qht, lambda c, v: put(4 + c, v))
+    for p in range(NP):
+        qht[p * 128:(p + 1) * 128, :] = qh_ref[:, p * 128:(p + 1) * 128].T
+    ffn_bwd_out(gb_ref, act_ref, lambda c, v: put(4 + c, v))
     acc_ref[...] = jnp.zeros_like(acc_ref)
     for c in range(4):
         before(c)
@@ -639,14 +630,16 @@
     dc = LaneSlots(act_ref)
     out_bwd(gb_ref, w.at[3], qct_ref, slc_ref, dc, vt_ref, functools.partial(put, 8))
     attn_bwd(q_ref, kt_ref, v_ref, dc, vt_ref, p_ref, q_ref, k_ref, v_ref, lambda p: None)
-    qkv_bwd(qi_ref, qct_ref, x_ref, w, q_ref, k_ref, v_ref, hid_ref, acc_ref, lambda m, v: put(9 + m, v), vec_ref, b[0], iv[0])
+    qkv_bwd_x(x_ref, w, q_ref, k_ref, v_ref, hid_ref, acc_ref, vec_ref, iv[0])
+    for m, ref in enumerate((q_ref, k_ref, v_ref)):
+        put(9 + m, nn(qit_ref[...], lanes(ref)))
     gx_ref[...] = x_ref[...]
 
 
 def local(x, ct, length, ranges, weights, small):
     def vm(*s, d=BF):
         return pltpu.VMEM(s, d)
-    scratch = [vm(6, D, D), vm(L, D), vm(6, L, 128), vm(6, L, 128), vm(6, L, 128), vm(6, 128, L),
+    scratch = [vm(6, D, D), vm(D, L), vm(6, L, 128), vm(6, L, 128), vm(6, L, 128), vm(6, 128, L),
                vm(6, 128, L), vm(6, 128, L), vm(12, L, L), vm(6, 128, L), vm(D, L), vm(L, D),
                vm(L, D, d=F32), vm(L, 128, d=F32), vm(L, D, d=F32), vm(L, D), vm(L, D), vm(4, L, D), vm(4, L, D), vm(L, D, d=F32),
                vm(L, D), vm(D, D), pltpu.SemaphoreType.DMA, pltpu.SemaphoreType.DMA]

time: 193 us -> 163 us (0.84)
  Pallas kernels: 175 us -> 146 us
    pallas_call x1, Pallas kernels: 175 us -> 146 us  [fused(): pl.pallas_call(functools.partial(fused_kernel, n_dp), out_shape=outs, in_...]
where the time goes in v3:
time: 163 us
  Pallas kernels  146 us (90%)
  local copies, waits for them, and re-layouts  15.5 us (10%)
    pallas_call x1, Pallas kernels, fused(): pl.pallas_call(functools.partial(fused_kernel, n_dp), out_shape=outs, in_...  146 us
    unnamed x21, local copies, waits for them, and re-layouts  4.97 us

profile of v3, /device:TPU:0, one launch (start us, length us, event | category | flops | bytes accessed | tf_op | source)
XLA Modules:
  0.0 163.2 jit_solution(5715457905822939860)
XLA Ops:
  0.6 0.0 copy-start.4
  0.7 0.0 copy-start.7
  0.7 0.0 copy-start.5
  0.7 0.0 copy-start.6
  0.7 0.0 copy-start.8
  0.7 0.0 copy-start.3
  0.7 2.7 %copy_bitcast_fusion = (bf16[4,128,768]{2,1,0:T(8,128)(2,1)}, bf16[4,128,768]{2,1,0:T(8,128)(2,1)}) fusion(bf16[128,4,768]{2,1,0:T(4,128)(2,1)} %param.27, bf16[128,4,768]{2,1,0:T(4,128)(2,1)} %param.14), kind=kLoop, calls=%fused_computation.2 | loop fusion | bytes 3145728 | tf_op jit(solution)/shard_map/transpose | solution.py:577
  3.5 0.0 copy-done.7
  3.5 0.0 copy-done.8
  3.5 0.0 copy-done.3
  3.5 0.0 copy-done.4
  3.5 0.0 copy-done.5
  3.5 0.0 copy-done.6
  3.5 0.1 concatenate.3
  3.6 0.6 convert_element_type.12.sm
  4.2 145.8 %shard_map.229 = (bf16[4,128,768]{2,1,0:T(8,128)(2,1)}, bf16[4,128,768]{2,1,0:T(8,128)(2,1)}, bf16[12,96,768]{2,1,0:T(8,128)(2,1)}, f32[16,768]{1,0:T(8,128)}) custom-call(bf16[4,128,768]{2,1,0:T(8,128)(2,1)} %get-tuple-element.52.tok, bf16[4,128,768]{2,1,0:T(8,128)(2,1)} %get-tuple-element.51.cot, s32[4]{0:T(128)} %len_ref.1, s32[4]{0:T(128)} %rng_ref.1, ...), custom_call_target="tpu_custom_call" | custom-call | tf_op jit(solution)/shard_map/pallas_call | solution.py:568
  150.0 0.0 copy-start.1
  150.0 2.7 %copy.33 = bf16[128,4,768]{2,1,0:T(4,128)(2,1)} copy(bf16[128,4,768]{2,0,1:T(8,128)(2,1)} %bitcast.20) | data formatting | bytes 1572864
  152.7 0.0 copy-done.1
  152.7 0.1 convert_bitcast_fusion
  152.9 0.0 copy-start
  152.9 2.2 %copy.34 = f32[128,4,768]{2,1,0:T(4,128)} copy(f32[128,4,768]{2,0,1:T(8,128)S(1)} %convert_bitcast_fusion) | data formatting | bytes 3145728
  155.0 0.0 copy-start.2
  155.0 0.0 copy-done
  155.0 1.0 slice.40
  156.0 0.0 copy-done.2
  156.0 0.6 constant_dynamic-slice_fusion.4
  156.7 0.3 convert_element_type.15
  157.0 0.7 slice_bitcast_fusion
  157.7 0.6 fusion
  158.3 0.6 constant_dynamic-slice_fusion.2
  159.0 0.6 constant_dynamic-slice_fusion.1
  159.6 1.2 fusion.2
  160.8 0.1 reverse_bitcast_fusion
  160.9 1.1 copy.35
  162.0 0.7 dynamic_slice.27
  162.7 0.6 fusion.1
  (7 shorter events, 0.1 us)
Async XLA Ops:
  0.6 2.9 %copy-start.4 = (bf16[2,768]{1,0:T(2,128)(2,1)S(1)}, bf16[2,768]{1,0:T(2,128)(2,1)}, u32[]{:S(2)}) copy-start(bf16[2,768]{1,0:T(2,128)(2,1)} %param.18) | copy-start | bytes 9220
  0.7 2.8 %copy-start.7 = (bf16[768]{0:T(1024)(128)(2,1)S(1)}, bf16[768]{0:T(1024)(128)(2,1)}, u32[]{:S(2)}) copy-start(bf16[768]{0:T(1024)(128)(2,1)} %param.20) | copy-start | bytes 4612
  0.7 2.9 %copy-start.5 = (bf16[2,768]{1,0:T(2,128)(2,1)S(1)}, bf16[2,768]{1,0:T(2,128)(2,1)}, u32[]{:S(2)}) copy-start(bf16[2,768]{1,0:T(2,128)(2,1)} %param.21) | copy-start | bytes 9220
  0.7 2.9 %copy-start.6 = (bf16[2,768]{1,0:T(2,128)(2,1)S(1)}, bf16[2,768]{1,0:T(2,128)(2,1)}, u32[]{:S(2)}) copy-start(bf16[2,768]{1,0:T(2,128)(2,1)} %param.22) | copy-start | bytes 9220
  0.7 2.8 %copy-start.8 = (bf16[768]{0:T(1024)(128)(2,1)S(1)}, bf16[768]{0:T(1024)(128)(2,1)}, u32[]{:S(2)}) copy-start(bf16[768]{0:T(1024)(128)(2,1)} %param.26) | copy-start | bytes 4612
  0.7 2.8 %copy-start.3 = (bf16[3072]{0:T(1024)(128)(2,1)S(1)}, bf16[3072]{0:T(1024)(128)(2,1)}, u32[]{:S(2)}) copy-start(bf16[3072]{0:T(1024)(128)(2,1)} %param.24) | copy-start | bytes 18436
  150.0 2.7 %copy-start.1 = (bf16[4,128,768]{2,1,0:T(8,128)(2,1)S(1)}, bf16[4,128,768]{2,1,0:T(8,128)(2,1)}, u32[]{:S(2)}) copy-start(bf16[4,128,768]{2,1,0:T(8,128)(2,1)} %get-tuple-element.17) | copy-start | bytes 2359300
  152.9 2.2 %copy-start = (bf16[12,96,768]{2,1,0:T(8,128)(2,1)S(1)}, bf16[12,96,768]{2,1,0:T(8,128)(2,1)}, u32[]{:S(2)}) copy-start(bf16[12,96,768]{2,1,0:T(8,128)(2,1)} %get-tuple-element.18) | copy-start | bytes 5308420
  155.0 1.0 copy-start.2

commit v4 on v3

--- a/solution.py
+++ b/solution.py
@@ -27,7 +27,7 @@
     def it(r, c):
         f(pl.multiple_of(r * step, step))
         return c
-    lax.fori_loop(0, n // step, it, 0)
+    lax.fori_loop(0, n // step, it, 0, unroll=2)
 
 
 def mean(v):
@@ -63,14 +63,16 @@
 
 
 def attn_fwd(q_t, k_ref, v_t, p_ref, ctxt_ref, length):
-    live = lax.broadcasted_iota(jnp.int32, (L, L), 0) < length
+    dead = (lax.broadcasted_iota(jnp.int32, (L, 128), 0) >= length) & (lax.broadcasted_iota(jnp.int32, (L, 128), 1) == 0)
+    dead = jnp.where(dead, -1e9, 0.0).astype(BF)
+    one = (lax.broadcasted_iota(jnp.int32, (128, L), 0) == 0).astype(F32).astype(BF)
     low = lax.broadcasted_iota(jnp.int32, (128, L), 0) < 64
 
     def pair(p, c):
-        kp, qt, vt = k_ref[p], q_t[p], v_t[p]
+        kp, qt, vt = jnp.concatenate([k_ref[p], dead], axis=1), q_t[p], v_t[p]
         for t in range(2):
             qm = jnp.where(low if t == 0 else ~low, qt, jnp.zeros_like(qt))
-            s = jnp.where(live, nn(kp, qm), -1e9)
+            s = nn(kp, jnp.concatenate([qm, one], axis=0))
             e = jnp.exp(s - jnp.max(s, axis=0, keepdims=True))
             pr = (e * (1.0 / jnp.sum(e, axis=0, keepdims=True))).astype(BF)
             p_ref[2 * p + t] = pr
@@ -257,9 +259,9 @@
 V_WITH = 9
 
 
-def fused_kernel(n_dp, tok, cot, len_ref, rng_ref, wqkv, wo, win, wout, sm,
+def fused_kernel(n_dp, tok, cot, len_ref, rng_ref, wqkv, wo, win, wout, qvb, ob, gains, shifts, fib, fob,
                  outp, gxp, gw, vout,
-                 w, g, x_ref, ct_ref, qit_ref, q_ref, k_ref, v_ref, qt_ref, kt_ref, vt_ref, p_ref, ctxt_ref, qct_ref, slc_ref,
+                 sm, w, g, x_ref, ct_ref, qit_ref, q_ref, k_ref, v_ref, qt_ref, kt_ref, vt_ref, p_ref, ctxt_ref, qct_ref, slc_ref,
                  n1_ref, r1_ref, hid_ref, slh_ref, qh_ref, act_ref, dfac_ref, acc_ref, gb_ref, za, vec, vrecv, *rest):
     nb = n_dp.bit_length() - 1
     bufs, (wsem, locsem, a2s, a2r, gs_sem, gr_sem, zs_sem, zr_sem, vs_sem, vr_sem) = rest[:nb], rest[nb:]
@@ -419,6 +421,14 @@
     b = [jnp.full((1, 1), rng_ref[i], jnp.int32).astype(F32) * (1 / 16.0) for i in range(4)]
     iv = [1.0 / t for t in b]
     vec[0] = jnp.zeros_like(vec[0])
+    sm[0:2, :] = qvb[...].astype(F32)
+    sm[2:3, :] = ob[...].astype(F32).reshape(1, D)
+    sm[3:5, :] = gains[...].astype(F32)
+    sm[5:7, :] = shifts[...].astype(F32)
+    sm[7:8, :] = fob[...].astype(F32).reshape(1, D)
+    ffb = fib[...].astype(F32).reshape(1, F)
+    for c in range(4):
+        sm[8 + c:9 + c, :] = ffb[:, c * D:(c + 1) * D]
     v0 = vec.at[0]
 
     own_tok.wait()
@@ -428,12 +438,12 @@
         if j:
             to_seq_in(0, tok, x_ref, j - 1).wait_recv()
         qkv(x_ref, qit_ref, w, sm, q_ref, k_ref, v_ref, qt_ref, kt_ref, vt_ref, b[0], iv[0], seg(peers[j - 1] if j else z))
+    load_w(0, win_c(1)).start()
+    load_w(1, wout_c(1)).start()
     own_cot = pltpu.make_async_copy(cot.at[z], ct_ref.at[seg(z), :], locsem.at[1])
     own_cot.start()
     for j in (1, 2, 0):
         to_seq(1, cot, ct_ref, j).start()
-    load_w(0, win_c(1)).start()
-    load_w(1, wout_c(1)).start()
     attn_fwd(qt_ref, k_ref, vt_ref, p_ref, ctxt_ref, len_ref[z])
     load_w(3, wo).wait()
     out_proj(ctxt_ref, x_ref, w.at[3], sm, qct_ref, slc_ref, n1_ref, r1_ref, hid_ref, slh_ref, qh_ref, acc_ref, b[1], iv[1], b[2], iv[2])
@@ -556,7 +566,7 @@
     def vm(*s, d=BF):
         return pltpu.VMEM(s, d)
     dma = pltpu.SemaphoreType.DMA
-    scratch = [vm(6, D, D), vm(8, n_dp, rs, D), vm(L, D), vm(L, D), vm(D, L), vm(6, L, 128), vm(6, L, 128), vm(6, L, 128), vm(6, 128, L),
+    scratch = [vm(12, D, d=F32), vm(6, D, D), vm(8, n_dp, rs, D), vm(L, D), vm(L, D), vm(D, L), vm(6, L, 128), vm(6, L, 128), vm(6, L, 128), vm(6, 128, L),
                vm(6, 128, L), vm(6, 128, L), vm(12, L, L), vm(6, 128, L), vm(D, L), vm(L, D),
                vm(L, D, d=F32), vm(L, 128, d=F32), vm(L, D, d=F32), vm(L, D), vm(L, D), vm(4, L, D), vm(4, L, D), vm(L, D, d=F32),
                vm(L, D), vm(12, rs, D), vm(nb + 2, 16, D, d=F32), vm(nb + 2, 16, D, d=F32)]
@@ -566,25 +576,81 @@
     outs = [pos, pos, jax.ShapeDtypeStruct((12, rs, D), BF), jax.ShapeDtypeStruct((16, D), F32)]
     v, s, h = (pl.BlockSpec(memory_space=m) for m in (pltpu.VMEM, pltpu.SMEM, pl.ANY))
     return pl.pallas_call(
-        functools.partial(fused_kernel, n_dp), out_shape=outs, in_specs=[h, h, s, s, h, h, h, h, v], out_specs=[h, h, v, v],
+        functools.partial(fused_kernel, n_dp), out_shape=outs, in_specs=[h, h, s, s, h, h, h, h] + [v] * 6, out_specs=[h, h, v, v],
         scratch_shapes=scratch,
         compiler_params=pltpu.CompilerParams(collective_id=0, has_side_effects=True, vmem_limit_bytes=64 * 1024 * 1024 - 65536))(*args)
 
 
+def finish_kernel(n_dp, outp, gxp, gw, vec, out, gx, gqkv, gqvb, gwo, gob, gains, shifts, gwin, gfib, gwout, gfob,
+                  seq_in, gw_in, tmp, seq_out, gx_out, gw_out, isem, osem):
+    rs = D // n_dp
+    i = lax.axis_index("dp")
+    ins = [pltpu.make_async_copy(outp, seq_in.at[0], isem.at[0]), pltpu.make_async_copy(gw, gw_in, isem.at[1]),
+           pltpu.make_async_copy(gxp, seq_in.at[1], isem.at[2])]
+    for c in ins:
+        c.start()
+    outs = []
+
+    def send(src, dst):
+        c = pltpu.make_async_copy(src, dst, osem.at[len(outs)])
+        c.start()
+        outs.append(c)
+
+    v, fib = vec[0:8, :], vec[8:12, :]
+    mine, f = jnp.zeros((8, rs), F32), jnp.zeros((1, 4 * rs), F32)
+    per = D // (4 * rs)
+    for k in range(n_dp):
+        mine = jnp.where(i == k, v[:, k * rs:(k + 1) * rs], mine)
+        f = jnp.where(i == k, fib[k // per:k // per + 1, (k % per) * 4 * rs:(k % per + 1) * 4 * rs], f)
+    gqvb[...] = mine[0:2]
+    gob[...] = mine[2:3]
+    gains[...] = mine[3:5]
+    shifts[...] = mine[5:7]
+    gfob[...] = mine[7:8]
+    gfib[...] = f.reshape(4 * rs)
+    ins[0].wait()
+    for s in range(4):
+        tmp[:, s, :] = seq_in[0, s].astype(F32)
+    seq_out[...] = tmp[...].astype(BF)
+    send(seq_out, out)
+    ins[1].wait()
+    for k in range(12):
+        gw_out[k] = gw_in[k].astype(F32)
+        if k < 4:
+            send(gw_out.at[k], gwout.at[pl.ds(k * rs, rs), :])
+        elif k < 8:
+            send(gw_out.at[k], gwin.at[:, pl.ds((7 - k) * D, D)])
+        elif k == 8:
+            send(gw_out.at[k], gwo)
+        else:
+            send(gw_out.at[k], gqkv.at[k - 9])
+    ins[2].wait()
+    for s in range(4):
+        gx_out[:, s, :] = seq_in[1, s].astype(F32)
+    send(gx_out, gx)
+    for c in outs:
+        c.wait()
+
+
+def finish(n_dp, *args):
+    rs, seg = D // n_dp, L // 4
+    shapes = [((seg, 4, D), BF), ((seg, 4, D), F32)]
+    shapes += [(s, F32) for s in ((3, rs, D), (2, rs), (rs, D), (1, rs), (2, rs), (2, rs), (rs, F), (4 * rs,), (4 * rs, D), (1, rs))]
+    v, h = pl.BlockSpec(memory_space=pltpu.VMEM), pl.BlockSpec(memory_space=pl.ANY)
+    vm, dma = pltpu.VMEM, pltpu.SemaphoreType.DMA
+    return pl.pallas_call(
+        functools.partial(finish_kernel, n_dp), out_shape=[jax.ShapeDtypeStruct(s, d) for s, d in shapes], in_specs=[h, h, h, v],
+        out_specs=[h, h, h, v, h, v, v, v, h, v, h, v],
+        scratch_shapes=[vm((2, 4, seg, D), BF), vm((12, rs, D), BF), vm((seg, 4, D), F32), vm((seg, 4, D), BF), vm((seg, 4, D), F32),
+                        vm((12, rs, D), F32), dma((3,)), dma((14,))],
+        compiler_params=pltpu.CompilerParams(vmem_limit_bytes=60 * 1024 * 1024))(*args)
+
+
 def on_device(n_dp, tokens, lengths, ranges, qkv_weight, qv_bias, out_weight, out_bias, norm_gains, norm_shifts, ffn_in, ffn_in_bias,
               ffn_out, ffn_out_bias, cotangent):
-    small = jnp.concatenate([qv_bias, out_bias[None], norm_gains, norm_shifts, ffn_out_bias[None], ffn_in_bias.reshape(4, D)]).astype(F32)
-    out, gx, gw, vec = fused(n_dp, tokens.transpose(1, 0, 2), cotangent.transpose(1, 0, 2), lengths, ranges, qkv_weight, out_weight,
-                             ffn_in, ffn_out, small)
-    rs = D // n_dp
-    i = lax.axis_index("dp")
-    gw = gw.astype(F32)
-
-    def mine(v):
-        return lax.dynamic_slice_in_dim(v, i * rs, rs, axis=-1)
-    fib = lax.dynamic_slice(vec[8:12].reshape(-1), (i * 4 * rs,), (4 * rs,))
-    return (out.transpose(1, 0, 2), gx.transpose(1, 0, 2).astype(F32), gw[9:12], mine(vec[0:2]), gw[8], mine(vec[2]), mine(vec[3:5]),
-            mine(vec[5:7]), gw[7:3:-1].transpose(1, 0, 2).reshape(rs, F), fib, gw[0:4].reshape(4 * rs, D), mine(vec[7]))
+    res = finish(n_dp, *fused(n_dp, tokens.transpose(1, 0, 2), cotangent.transpose(1, 0, 2), lengths, ranges, qkv_weight, out_weight,
+                              ffn_in, ffn_out, qv_bias, out_bias, norm_gains, norm_shifts, ffn_in_bias, ffn_out_bias))
+    return tuple(r[0] if n in (5, 11) else r for n, r in enumerate(res))
 
 
 def local_kernel(x_ref, ct_ref, len_ref, rng_ref, w_ref, sm, gx_ref, g_ref, vec_ref, w, qit_ref, q_ref, k_ref, v_ref, qt_ref, kt_ref, vt_ref,

time: 163 us -> 155 us (0.951)
  local copies, waits for them, and re-layouts: 15.5 us -> 2.71 us
  Pallas kernels: 146 us -> 152 us
    pallas_call x0 -> x1, Pallas kernels: none -> 5.91 us  [finish(): pl.pallas_call(functools.partial(finish_kernel, n_dp), out_shape=[jax.Sha...]
    unnamed x21 -> x0, local copies, waits for them, and re-layouts: 4.97 us -> none
    dynamic_slice x6 -> x0, local copies, waits for them, and re-layouts: 3.72 us -> none  [the longest x5 3.07 us: mine(): return lax.dynamic_slice_in_dim(v, i * rs, rs, axis=-1)]
    slice x5 -> x0, local copies, waits for them, and re-layouts: 2.16 us -> none  [the longest x1 1.17 us: on_device(): gw[0:4].reshape(4 * rs, D)]
where the time goes in v4:
time: 155 us
  Pallas kernels  152 us (98%)
  local copies, waits for them, and re-layouts  2.71 us (2%)
    pallas_call x1, Pallas kernels, fused(): pl.pallas_call(functools.partial(fused_kernel, n_dp), out_shape=outs, in_...  146 us
    pallas_call x1, Pallas kernels, finish(): pl.pallas_call(functools.partial(finish_kernel, n_dp), out_shape=[jax.Sha...  5.91 us

profile of v4, /device:TPU:0, one launch (start us, length us, event | category | flops | bytes accessed | tf_op | source)
XLA Modules:
  0.0 155.1 jit_solution(17695117229199333331)
XLA Ops:
  0.6 2.7 %copy_bitcast_fusion = (bf16[4,128,768]{2,1,0:T(8,128)(2,1)}, bf16[4,128,768]{2,1,0:T(8,128)(2,1)}) fusion(bf16[128,4,768]{2,1,0:T(4,128)(2,1)} %param.27, bf16[128,4,768]{2,1,0:T(4,128)(2,1)} %param.14), kind=kLoop, calls=%fused_computation | loop fusion | bytes 3145728 | tf_op jit(solution)/shard_map/transpose | solution.py:651
  3.4 145.6 %shard_map.229 = (bf16[4,128,768]{2,1,0:T(8,128)(2,1)}, bf16[4,128,768]{2,1,0:T(8,128)(2,1)}, bf16[12,96,768]{2,1,0:T(8,128)(2,1)}, f32[16,768]{1,0:T(8,128)}) custom-call(bf16[4,128,768]{2,1,0:T(8,128)(2,1)} %get-tuple-element.45.tok, bf16[4,128,768]{2,1,0:T(8,128)(2,1)} %get-tuple-element.44.cot, s32[4]{0:T(128)} %len_ref.1, s32[4]{0:T(128)} %rng_ref.1, ...), custom_call_target="tpu_custom_call" | custom-call | tf_op jit(solution)/shard_map/pallas_call | solution.py:578
  149.0 5.9 %shard_map.230 = (bf16[128,4,768]{2,1,0:T(4,128)(2,1)}, f32[128,4,768]{2,1,0:T(4,128)}, f32[3,96,768]{2,1,0:T(8,128)}, f32[2,96]{1,0:T(2,128)}, f32[96,768]{1,0:...) custom-call(bf16[4,128,768]{2,1,0:T(8,128)(2,1)} %get-tuple-element., ...), custom_call_target="tpu_custom_call" | custom-call | tf_op jit(solution)/shard_map/pallas_call | solution.py:641

commit v5 on v4

--- a/solution.py
+++ b/solution.py
@@ -405,12 +405,12 @@
             vcopy(nb + 2).wait_recv()
 
     for m in range(3):
-        load_w(m, wqkv.at[m]).start()
+        load_w(m, wqkv.at[m]).start(priority=1)
     own_tok = pltpu.make_async_copy(tok.at[z], x_ref.at[seg(z), :], locsem.at[0])
     own_tok.start()
-    load_w(3, wo).start()
-    load_w(4, win_c(0)).start()
-    load_w(5, wout_c(0)).start()
+    load_w(3, wo).start(priority=1)
+    load_w(4, win_c(0)).start(priority=1)
+    load_w(5, wout_c(0)).start(priority=1)
     barrier = pltpu.get_barrier_semaphore()
     others = [at(buddy[b], z) for b in range(nb)] + [at(dp, p) for p in peers]
     for o in others:
@@ -438,8 +438,8 @@
         if j:
             to_seq_in(0, tok, x_ref, j - 1).wait_recv()
         qkv(x_ref, qit_ref, w, sm, q_ref, k_ref, v_ref, qt_ref, kt_ref, vt_ref, b[0], iv[0], seg(peers[j - 1] if j else z))
-    load_w(0, win_c(1)).start()
-    load_w(1, wout_c(1)).start()
+    load_w(0, win_c(1)).start(priority=1)
+    load_w(1, wout_c(1)).start(priority=1)
     own_cot = pltpu.make_async_copy(cot.at[z], ct_ref.at[seg(z), :], locsem.at[1])
     own_cot.start()
     for j in (1, 2, 0):
@@ -459,8 +459,8 @@
     def fwd_done(c):
         @pl.when(c < 2)
         def _():
-            load_w(w_slot(c), win_c(c + 2)).start()
-            load_w(w_slot(c) + 1, wout_c(c + 2)).start()
+            load_w(w_slot(c), win_c(c + 2)).start(priority=1)
+            load_w(w_slot(c) + 1, wout_c(c + 2)).start(priority=1)
 
     ffn_fwd(qh_ref, w, sm, act_ref, dfac_ref, acc_ref, b[3], iv[3], fwd_wait, fwd_done)
     own_cot.wait()
@@ -508,11 +508,11 @@
         ffn_bwd_in(c, gb_ref, w.at[s], w.at[s + 1], dfac_ref, acc_ref, qht, functools.partial(put, 4 + j), v0)
         red(4 + j, 0).start()
         if j < 2:
-            load_w(s, win_c(c - 2)).start()
-            load_w(s + 1, wout_c(c - 2)).start()
+            load_w(s, win_c(c - 2)).start(priority=1)
+            load_w(s + 1, wout_c(c - 2)).start(priority=1)
         if j == 2:
-            load_w(0, wqkv.at[0]).start()
-            load_w(1, wqkv.at[1]).start()
+            load_w(0, wqkv.at[0]).start(priority=1)
+            load_w(1, wqkv.at[1]).start(priority=1)
         at_point(f"f{j}")
     ln1_bwd(acc_ref, hid_ref, slh_ref, n1_ref, r1_ref, sm, gb_ref, v0)
     at_point("ln")

time: 155 us -> 155 us (level)
  no operation moved by 1% of the time
where the time goes in v5:
time: 155 us
  Pallas kernels  152 us (98%)
  local copies, waits for them, and re-layouts  2.71 us (2%)
    pallas_call x1, Pallas kernels, fused(): pl.pallas_call(functools.partial(fused_kernel, n_dp), out_shape=outs, in_...  146 us
    pallas_call x1, Pallas kernels, finish(): pl.pallas_call(functools.partial(finish_kernel, n_dp), out_shape=[jax.Sha...  5.91 us

profile of v5, /device:TPU:0, one launch (start us, length us, event | category | flops | bytes accessed | tf_op | source)
XLA Modules:
  0.0 155.1 jit_solution(5294172825800129560)
XLA Ops:
  0.6 2.7 %copy_bitcast_fusion = (bf16[4,128,768]{2,1,0:T(8,128)(2,1)}, bf16[4,128,768]{2,1,0:T(8,128)(2,1)}) fusion(bf16[128,4,768]{2,1,0:T(4,128)(2,1)} %param.27, bf16[128,4,768]{2,1,0:T(4,128)(2,1)} %param.14), kind=kLoop, calls=%fused_computation | loop fusion | bytes 3145728 | tf_op jit(solution)/shard_map/transpose | solution.py:651
  3.4 145.6 %shard_map.229 = (bf16[4,128,768]{2,1,0:T(8,128)(2,1)}, bf16[4,128,768]{2,1,0:T(8,128)(2,1)}, bf16[12,96,768]{2,1,0:T(8,128)(2,1)}, f32[16,768]{1,0:T(8,128)}) custom-call(bf16[4,128,768]{2,1,0:T(8,128)(2,1)} %get-tuple-element.45.tok, bf16[4,128,768]{2,1,0:T(8,128)(2,1)} %get-tuple-element.44.cot, s32[4]{0:T(128)} %len_ref.1, s32[4]{0:T(128)} %rng_ref.1, ...), custom_call_target="tpu_custom_call" | custom-call | tf_op jit(solution)/shard_map/pallas_call | solution.py:578
  149.0 5.9 %shard_map.230 = (bf16[128,4,768]{2,1,0:T(4,128)(2,1)}, f32[128,4,768]{2,1,0:T(4,128)}, f32[3,96,768]{2,1,0:T(8,128)}, f32[2,96]{1,0:T(2,128)}, f32[96,768]{1,0:...) custom-call(bf16[4,128,768]{2,1,0:T(8,128)(2,1)} %get-tuple-element., ...), custom_call_target="tpu_custom_call" | custom-call | tf_op jit(solution)/shard_map/pallas_call | solution.py:641

commit v6 on v5

--- a/solution.py
+++ b/solution.py
@@ -240,8 +240,7 @@
 
 MESH = pl.DeviceIdType.MESH
 SCHEDULE = {
-    "f0": [(0, 0)],
-    "f1": [(0, 1)],
+    "fo": [(0, 0), (0, 1)],
     "f2": [(0, 4)],
     "ln": [(1, 0), (0, 5)],
     "a0": [(1, 1)],

time: 155 us -> 157 us (1.013)
  no operation moved by 1% of the time
where the time goes in v6:
time: 157 us; the launch traced here: 156 us
  Pallas kernels  153 us (97%)
  local copies, waits for them, and re-layouts  2.71 us (2%)
    pallas_call x1, Pallas kernels, fused(): pl.pallas_call(functools.partial(fused_kernel, n_dp), out_shape=outs, in_...  147 us
    pallas_call x1, Pallas kernels, finish(): pl.pallas_call(functools.partial(finish_kernel, n_dp), out_shape=[jax.Sha...  5.91 us

profile of v6, /device:TPU:0, one launch (start us, length us, event | category | flops | bytes accessed | tf_op | source)
XLA Modules:
  0.0 156.3 jit_solution(14614907504284595135)
XLA Ops:
  0.6 2.7 %copy_bitcast_fusion = (bf16[4,128,768]{2,1,0:T(8,128)(2,1)}, bf16[4,128,768]{2,1,0:T(8,128)(2,1)}) fusion(bf16[128,4,768]{2,1,0:T(4,128)(2,1)} %param.27, bf16[128,4,768]{2,1,0:T(4,128)(2,1)} %param.14), kind=kLoop, calls=%fused_computation | loop fusion | bytes 3145728 | tf_op jit(solution)/shard_map/transpose | solution.py:650
  3.4 146.8 %shard_map.229 = (bf16[4,128,768]{2,1,0:T(8,128)(2,1)}, bf16[4,128,768]{2,1,0:T(8,128)(2,1)}, bf16[12,96,768]{2,1,0:T(8,128)(2,1)}, f32[16,768]{1,0:T(8,128)}) custom-call(bf16[4,128,768]{2,1,0:T(8,128)(2,1)} %get-tuple-element.45.tok, bf16[4,128,768]{2,1,0:T(8,128)(2,1)} %get-tuple-element.44.cot, s32[4]{0:T(128)} %len_ref.1, s32[4]{0:T(128)} %rng_ref.1, ...), custom_call_target="tpu_custom_call" | custom-call | tf_op jit(solution)/shard_map/pallas_call | solution.py:577
  150.2 5.9 %shard_map.230 = (bf16[128,4,768]{2,1,0:T(4,128)(2,1)}, f32[128,4,768]{2,1,0:T(4,128)}, f32[3,96,768]{2,1,0:T(8,128)}, f32[2,96]{1,0:T(2,128)}, f32[96,768]{1,0:...) custom-call(bf16[4,128,768]{2,1,0:T(8,128)(2,1)} %get-tuple-element., ...), custom_call_target="tpu_custom_call" | custom-call | tf_op jit(solution)/shard_map/pallas_call | solution.py:640
